TPU v7x, 128 devices: a whole 4x4x4 slice. The times are simulated.
128 devices in a mesh: sect: 16 (over y, x), lane: 8 (over z, core).
Axes of the slice: x: 4, y: 4, z: 4, core: 2. Of those that a mesh axis runs over, the one named last changes fastest.
Arguments:
- atm_state: bfloat16 [524288, 512], P(('sect', 'lane')), may hold values from -6 to 6
- profile: float32 [128], replicated, may hold values from 0.02 to 0.5
- mixing: bfloat16 [4, 128, 128], replicated, may hold values from -0.5 to 0.5
- radiation: float32 [4, 524288], P(None, ('sect', 'lane')), may hold values from 0 to 1
- ocean_mask: int32 [524288], P(('sect', 'lane')), may hold values 0 or 1
- tile_src: int32 [32768, 4], P(('sect', 'lane')), may hold values from 0 to 127, all different within a row; in each aligned block of 256 rows (0 to 255, 256 to 511, ...) at most 16 rows name the same one
- tile_elem: int32 [32768, 4], P(('sect', 'lane')), may hold values from 0 to 255
- remap_w: float32 [32768, 64, 128], P(('sect', 'lane')), may hold values from 0.05 to 1
- slope_class: int32 [32768, 128], P(('sect', 'lane')), may hold values from 0 to 7
- aspect_class: int32 [32768, 128], P(('sect', 'lane')), may hold values from 0 to 7
- sky_view: float32 [32768, 128], P(('sect', 'lane')), may hold values from 0.6 to 1
- albedo: float32 [32768, 128], P(('sect', 'lane')), may hold values from 0.1 to 0.4
- sun_cos: float32 [32768], P(('sect', 'lane')), may hold values from 0.25 to 1
- sun_azimuth: float32 [32768], P(('sect', 'lane')), may hold values from -3.140625 to 3.140625
Outputs:
- atm_out: bfloat16 [524288, 512], P(('sect', 'lane'))
- land_temp: float32 [32768, 128], P(('sect', 'lane'))
- col_flux: float32 [8, 524288], P(None, ('sect', 'lane'))
Inputs may be any that keep to these rules, and one draw needn't show every extreme that they name: `tile_src`: each tile names 4 different atmosphere devices; among the tiles of one device no atmosphere device is named more than 16 times, a bound that some block reaches.
All inputs are finite; a program needn't handle non-finite values. No bound on the sum of `ocean_mask` on one device may be relied on, other than what follows from the above.
Results may differ from a plain program's by a relative error of at most 0.001.
The roundings to bfloat16 on the way count: a program that leaves them out, or rounds other values in their place, can miss the bound.
Values sent between devices are 32-bit elements; how exact they have to be, the bound alone decides.
No kernel may reach another device: no remote copies, remote signals or barrier semaphores. Data moves between devices by JAX's collectives and lax.ppermute only.
A program may use at most 128 MiB of HBM per device.

v0:
```python
import functools
import math

import jax
import jax.numpy as jnp
from jax import lax
from jax.experimental import pallas as pl
from jax.experimental.pallas import tpu as pltpu
from jax.sharding import PartitionSpec as P

GLL = 16
LEV = 128
NV = 4
NF = 8
SUB = 4
NEWTON = 2
NASPECT = 8
CAP = 16
UNIT = 128
REF = 4
KDIM = REF * GLL
AXES = ("sect", "lane")

F32 = jnp.float32
BF16 = jnp.bfloat16
I32 = jnp.int32
MIB = 1 << 20


def iota(shape, axis):
    return lax.broadcasted_iota(I32, shape, axis)


def matmul(left, right):
    return jnp.dot(left, right, preferred_element_type=F32)


def matmul_nt(left, right):
    return lax.dot_general(left, right, (((1,), (1,)), ((), ())), preferred_element_type=F32)


def flag(condition):
    return jnp.where(condition, 1.0, 0.0).astype(BF16)


def high_low(values):
    high = values.astype(BF16).astype(F32)
    return high, values - high


def pair(values):
    high, low = high_low(values)
    return jnp.concatenate([high.astype(BF16), low.astype(BF16)], axis=1)


def fold(values):
    half = values.shape[1] // 2
    return values[:, :half] + values[:, half:]


def block_swap(values):
    cube = values.reshape(values.shape[0] // 8, 8, 128)
    rows, lanes = iota(cube.shape, 1), iota(cube.shape, 2)
    for step in range(3):
        reach = 1 << step
        row_bit, chunk_bit = (rows >> step) & 1, (lanes >> (4 + step)) & 1
        up = pltpu.roll(pltpu.roll(cube, 8 - reach, 1), 16 * reach, 2)
        if reach == 4:
            moved = up
        else:
            down = pltpu.roll(pltpu.roll(cube, reach, 1), 128 - 16 * reach, 2)
            moved = jnp.where(chunk_bit == 1, up, down)
        cube = jnp.where(row_bit == chunk_bit, cube, moved)
    return cube.reshape(values.shape)


def drivers(fields):
    air_temp = 1.0 + 0.05 * jnp.tanh(fields[0])
    air_humid = 0.02 / (1.0 + jnp.exp(-fields[1]))
    wind_speed = jnp.sqrt(1.0 + fields[2] * fields[2] + fields[3] * fields[3])
    return (
        air_temp,
        air_humid,
        wind_speed,
        1.5 * fields[4],
        0.5 * fields[5],
        0.6 + 0.3 * fields[6],
        fields[7],
    )


def flux_list(surface, fields, driven, absorbed, reflected, wetness):
    air_temp, air_humid, wind_speed = driven[:3]
    heat_coef = 0.1 * wind_speed
    vapor_coef = 0.25 * wind_speed * wetness
    saturation = 0.02 * jnp.exp(17.0 * (surface - 1.0))
    sensible = heat_coef * (surface - air_temp)
    latent = vapor_coef * (saturation - air_humid)
    square = surface * surface
    upward = 0.95 * (square * square)
    drag = 0.05 * wind_speed
    return [
        sensible,
        latent,
        upward,
        reflected,
        drag * fields[2],
        drag * fields[3],
        0.4 * latent,
        absorbed - upward - sensible - latent,
    ]


def route_kernel(src_ref, elem_ref, want_ref, row_ref, col_ref):
    devices, tiles = want_ref.shape[0], src_ref.shape[1]
    owner = iota((devices, tiles), 0)
    slot = iota((128, tiles), 0)
    earlier = flag(iota((tiles, tiles), 0) < iota((tiles, tiles), 1))
    base = jnp.zeros((devices, 1), F32)
    wanted = jnp.zeros((devices, 128), F32)
    places = []
    for ref in range(REF):
        source = src_ref[ref : ref + 1, :]
        hit = owner == source
        onehot = flag(hit)
        before = matmul(onehot, earlier) + base
        rank = jnp.sum(jnp.where(hit, before, 0.0), axis=0, keepdims=True)
        base = base + jnp.sum(jnp.where(hit, 1.0, 0.0), axis=1, keepdims=True)
        rank = rank.astype(I32)
        value = (elem_ref[ref : ref + 1, :] + 1).astype(F32)
        table = jnp.where(slot == rank, value, 0.0).astype(BF16)
        wanted = wanted + matmul_nt(onehot, table)
        places.append(source * CAP + rank)
    want_ref[...] = wanted.astype(I32) - 1
    for ref in range(REF):
        row_ref[ref : ref + 1, :] = places[ref]
    stacked = jnp.concatenate(places + places, axis=0).astype(F32)
    col_ref[...] = jnp.transpose(stacked).astype(I32)


def forcing_kernel(profile_ref, state_ref, radiation_ref, forcing_ref, blocks_ref):
    whole = profile_ref[...]
    first = whole.astype(BF16).astype(F32)
    second = (whole - first).astype(BF16).astype(F32)
    third = whole - first - second
    rows = iota((32, LEV), 0)
    piece = jnp.where(rows < 8, first, jnp.where(rows < 16, second, jnp.where(rows < 24, third, 0.0)))
    spread = jnp.concatenate(
        [jnp.where((rows & 7) == variable, piece, 0.0) for variable in range(NV)], axis=1
    ).astype(BF16)
    sums = matmul_nt(spread, state_ref[...])
    means = sums[0:8] + sums[8:16] + sums[16:24]
    forcing = jnp.concatenate([means[0:NV], radiation_ref[...]], axis=0)
    forcing_ref[...] = forcing
    columns = forcing.shape[1]
    stacked = jnp.concatenate(
        [forcing[:, start : start + 128] for start in range(0, columns, 128)], axis=0
    )
    blocks_ref[...] = pair(block_swap(stacked))


def reply_kernel(incoming_ref, blocks_ref, reply_ref):
    devices, elements = incoming_ref.shape[0], blocks_ref.shape[0]
    element = iota((devices, elements), 1)
    blocks = blocks_ref[...]
    incoming = incoming_ref[...]
    for slot in range(CAP):
        select = flag(element == incoming[:, slot : slot + 1])
        reply_ref[pl.ds(slot, devices, stride=CAP), :] = fold(matmul(select, blocks))


def mix_kernel(mixing_ref, state_ref, mixed_ref):
    zero = jnp.zeros((LEV, LEV), BF16)
    operator = jnp.concatenate(
        [
            jnp.concatenate([mixing_ref[0], zero], axis=1),
            jnp.concatenate([zero, mixing_ref[1]], axis=1),
        ],
        axis=0,
    )
    rows = state_ref.shape[0]
    part = 256
    for start in range(0, rows, part):
        state = state_ref[start : start + part, :]
        for iteration in range(SUB):
            update = matmul(state, operator)
            state = (state.astype(F32) + 0.25 * jnp.tanh(update)).astype(BF16)
        mixed_ref[start : start + part, :] = state


def ocean_kernel(forcing_ref, mask_ref, ocean_ref):
    fields = [forcing_ref[index : index + 1, :] for index in range(NF)]
    driven = drivers(fields)
    shortwave = driven[3] + driven[4]
    absorbed = 0.94 * shortwave + 0.95 * driven[5]
    one = jnp.ones_like(fields[0])
    fluxes = flux_list(one, fields, driven, absorbed, 0.06 * shortwave, one)
    mask = mask_ref[...].astype(F32)
    for index in range(NF):
        ocean_ref[index : index + 1, :] = mask * fluxes[index]


def land_kernel(
    arrived_ref,
    row_ref,
    col_ref,
    w_ref,
    incidence_ref,
    sky_ref,
    albedo_ref,
    temp_ref,
    outgoing_ref,
    need_ref,
    both_ref,
    raw_ref,
    total_ref,
):
    step = pl.program_id(0)
    slots = arrived_ref.shape[0]
    tiles = row_ref.shape[1]
    step_tiles = w_ref.shape[0] // KDIM
    groups = step_tiles // 4

    @pl.when(step == 0)
    def _():
        arrived = pair(arrived_ref[...])
        slot = iota((tiles, slots), 1)
        for ref in range(REF):
            pick = flag(slot == col_ref[:, ref : ref + 1])
            need_ref[pl.ds(ref, tiles, stride=REF), :] = fold(matmul(pick, arrived))
        need_ref[...] = block_swap(need_ref[...])

    left = iota((8, 128), 1) < KDIM
    zero = jnp.zeros((8, 128), F32)
    lane = iota((16, 256), 1)
    ones = jnp.where((lane >> 6) == iota((16, 256), 0), 1.0, 0.0)

    for group in range(groups):
        weights = pair(w_ref[group * 256 : (group + 1) * 256, :])
        both_ref[pl.ds(pl.multiple_of(step * (groups * 256), 256) + group * 256, 256), :] = weights
        start = pl.multiple_of(step * (groups * 16), 16) + group * 16
        need = need_ref[pl.ds(start, 16), :]
        rows = []
        for part in high_low(need):
            for half in range(2):
                block = part[half * 8 : half * 8 + 8]
                for masked in (jnp.where(left, block, 0.0), jnp.where(left, 0.0, block)):
                    rows.append(
                        jnp.concatenate([masked, zero] if half == 0 else [zero, masked], axis=1)
                    )
        rows.append(ones)
        product = fold(matmul(jnp.concatenate(rows, axis=0).astype(BF16), weights))
        raw_ref[pl.ds(pl.multiple_of(step * (groups * 32), 32) + group * 32, 32), :] = (
            product[0:32] + product[32:64]
        )
        total_ref[pl.ds(pl.multiple_of(step * (groups * 8), 8) + group * 8, 8), :] = product[64:72]

    @pl.when(step == pl.num_programs(0) - 1)
    def _():
        sums = jnp.concatenate(
            [
                total_ref[index * 8 : index * 8 + 4, :]
                for index in range(tiles // 4)
            ],
            axis=0,
        )
        inverse = 1.0 / sums
        fields = [raw_ref[pl.ds(index, tiles, stride=NF), :] * inverse for index in range(NF)]
        driven = drivers(fields)
        air_temp, air_humid, wind_speed, direct_sw, diffuse_sw, longwave, wetness = driven
        sky, albedo = sky_ref[...], albedo_ref[...]
        shortwave = direct_sw * incidence_ref[...] + diffuse_sw * sky
        absorbed = (1.0 - albedo) * shortwave + 0.95 * longwave * sky
        heat_coef = 0.1 * wind_speed
        vapor_coef = 0.25 * wind_speed * wetness
        surface = air_temp
        for iteration in range(NEWTON):
            saturation = 0.02 * jnp.exp(17.0 * (surface - 1.0))
            square = surface * surface
            imbalance = (
                absorbed
                - 0.95 * (square * square)
                - heat_coef * (surface - air_temp)
                - vapor_coef * (saturation - air_humid)
            )
            derivative = -3.8 * (square * surface) - heat_coef - 17.0 * vapor_coef * saturation
            surface = surface - imbalance / derivative
        temp_ref[...] = surface
        fluxes = flux_list(surface, fields, driven, absorbed, albedo * shortwave, wetness)
        for index in range(NF):
            raw_ref[pl.ds(index, tiles, stride=NF), :] = fluxes[index] * inverse

        def give(group, carry):
            flux = raw_ref[pl.ds(pl.multiple_of(group * 32, 32), 32), :]
            high, low = high_low(flux)
            stacked = jnp.concatenate([high, low], axis=0).astype(BF16)
            stacked = jnp.concatenate([stacked, stacked], axis=1)
            weights = both_ref[pl.ds(pl.multiple_of(group * 256, 256), 256), :]
            product = matmul_nt(stacked, weights)
            product = product[0:32] + product[32:64]
            need_ref[pl.ds(pl.multiple_of(group * 16, 16), 16), :] = jnp.concatenate(
                [
                    jnp.where(left, product[0:8, 0:128], product[8:16, 0:128]),
                    jnp.where(left, product[16:24, 128:256], product[24:32, 128:256]),
                ],
                axis=0,
            )
            return carry

        lax.fori_loop(0, tiles // 4, give, 0, unroll=8)
        need_ref[...] = block_swap(need_ref[...])
        given = jnp.concatenate(
            [pair(need_ref[pl.ds(ref, tiles, stride=REF), :]) for ref in range(REF)], axis=0
        )
        size = 256

        def place(index, carry):
            start = pl.multiple_of(index * size, size)
            slot = iota((size, tiles), 0) + start
            pick = jnp.concatenate(
                [flag(slot == row_ref[ref : ref + 1, :]) for ref in range(REF)], axis=1
            )
            outgoing_ref[pl.ds(start, size), :] = fold(matmul(pick, given))
            return carry

        lax.fori_loop(0, slots // size, place, 0, unroll=2)


def finish_kernel(returned_ref, incoming_ref, ocean_ref, mixed_ref, kept_ref, out_ref, flux_ref):
    del kept_ref
    step = pl.program_id(0)
    devices = incoming_ref.shape[0]
    elements = flux_ref.shape[1] // GLL

    @pl.when(step == 0)
    def _():
        incoming = jnp.transpose(incoming_ref[...].astype(F32)).astype(I32)
        element = iota((elements, devices), 0)
        part = jnp.zeros((elements, 256), F32)
        for slot in range(0, CAP, 2):
            select = jnp.concatenate(
                [flag(element == incoming[slot + extra : slot + extra + 1, :]) for extra in range(2)],
                axis=1,
            )
            values = jnp.concatenate(
                [
                    pair(returned_ref[pl.ds(slot + extra, devices, stride=CAP), :])
                    for extra in range(2)
                ],
                axis=0,
            )
            part = part + matmul(select, values)
        swapped = block_swap(fold(part))
        for index in range(elements // 8):
            columns = slice(index * 128, index * 128 + 128)
            flux_ref[:, columns] = swapped[index * 8 : index * 8 + 8] + ocean_ref[:, columns]

    rows = out_ref.shape[0]
    lane = iota((128, 128), 1)
    for start in range(0, rows, 128):
        begin = pl.multiple_of(step * rows, rows) + start
        turned = jnp.transpose(flux_ref[:, pl.ds(begin, 128)])
        for half, index in ((0, 0), (1, 6)):
            lanes = slice(half * 128, half * 128 + 128)
            added = jnp.where(lane == 0, 0.1 * turned[:, index : index + 1], 0.0)
            state = mixed_ref[start : start + 128, lanes].astype(F32)
            out_ref[start : start + 128, lanes] = (state + added).astype(BF16)


def whole(*shape):
    return pl.BlockSpec(shape, lambda *_: (0,) * len(shape))


def params(mebibytes, axes=0):
    return pltpu.CompilerParams(
        vmem_limit_bytes=mebibytes * MIB,
        dimension_semantics=("arbitrary",) * axes if axes else None,
    )


def cost(flops, moved, hard=0):
    return pl.CostEstimate(flops=int(flops), bytes_accessed=int(moved), transcendentals=int(hard))


def mix(mixing, atm_state, half, place_half, width):
    columns = atm_state.shape[0]
    rows = 512
    return pl.pallas_call(
        mix_kernel,
        grid=(columns // rows,),
        in_specs=[
            pl.BlockSpec((2, LEV, LEV), lambda i: (half, 0, 0)),
            pl.BlockSpec((rows, 256), lambda i: (i, half)),
        ],
        out_specs=pl.BlockSpec((rows, 256), lambda i: (i, place_half)),
        out_shape=jax.ShapeDtypeStruct((columns, width), BF16),
        compiler_params=params(16, 1),
        cost_estimate=cost(columns * 256 * 256 * 2 * SUB, columns * 256 * 4, columns * 256 * SUB),
    )(mixing, atm_state)


def on_device(
    atm_state,
    profile,
    mixing,
    radiation,
    ocean_mask,
    tile_src,
    tile_elem,
    remap_w,
    slope_class,
    aspect_class,
    sky_view,
    albedo,
    sun_cos,
    sun_azimuth,
):
    devices = lax.axis_size("sect") * lax.axis_size("lane")
    columns = atm_state.shape[0]
    elements = columns // GLL
    tiles = tile_src.shape[0]
    slots = devices * CAP
    requests = tiles * REF

    wanted, slot_row, slot_col = pl.pallas_call(
        route_kernel,
        out_shape=(
            jax.ShapeDtypeStruct((devices, 128), I32),
            jax.ShapeDtypeStruct((REF, tiles), I32),
            jax.ShapeDtypeStruct((tiles, 2 * REF), I32),
        ),
        compiler_params=params(16),
    )(tile_src.T, tile_elem.T)
    incoming = lax.all_to_all(wanted, AXES, split_axis=0, concat_axis=0, tiled=True)

    rows = 512
    forcing, blocks = pl.pallas_call(
        forcing_kernel,
        grid=(columns // rows,),
        in_specs=[
            whole(1, LEV),
            pl.BlockSpec((rows, NV * LEV), lambda i: (i, 0)),
            pl.BlockSpec((4, rows), lambda i: (0, i)),
        ],
        out_specs=(
            pl.BlockSpec((NF, rows), lambda i: (0, i)),
            pl.BlockSpec((rows // GLL, 256), lambda i: (i, 0)),
        ),
        out_shape=(
            jax.ShapeDtypeStruct((NF, columns), F32),
            jax.ShapeDtypeStruct((elements, 256), BF16),
        ),
        compiler_params=params(16, 1),
        cost_estimate=cost(columns * 512 * 32 * 2, columns * 1024),
    )(profile.reshape(1, LEV), atm_state, radiation)

    reply = pl.pallas_call(
        reply_kernel,
        out_shape=jax.ShapeDtypeStruct((slots, 128), F32),
        compiler_params=params(16),
        cost_estimate=cost(slots * 256 * 256 * 2, slots * 512),
    )(incoming, blocks)
    arrived = lax.all_to_all(
        reply.reshape(devices, CAP, 128), AXES, split_axis=0, concat_axis=0, tiled=True
    ).reshape(slots, 128)

    kept = mix(mixing, atm_state, 1, 1, NV * LEV)
    cosine = sun_cos[:, None]
    sine = jnp.sqrt(1.0 - cosine * cosine)
    slope_angle = slope_class.astype(F32) * 0.1
    aspect_angle = aspect_class.astype(F32) * (2.0 * math.pi / NASPECT)
    incidence = (
        jnp.maximum(
            0.0,
            jnp.cos(slope_angle) * cosine
            + jnp.sin(slope_angle) * sine * jnp.cos(sun_azimuth[:, None] - aspect_angle),
        )
        / cosine
    )

    step_tiles = 32
    land_temp, outgoing = pl.pallas_call(
        land_kernel,
        grid=(tiles // step_tiles,),
        in_specs=[
            whole(slots, 128),
            whole(REF, tiles),
            whole(tiles, 2 * REF),
            pl.BlockSpec((step_tiles * KDIM, UNIT), lambda i: (i, 0)),
            whole(tiles, UNIT),
            whole(tiles, UNIT),
            whole(tiles, UNIT),
        ],
        out_specs=(whole(tiles, UNIT), whole(slots, 128)),
        out_shape=(
            jax.ShapeDtypeStruct((tiles, UNIT), F32),
            jax.ShapeDtypeStruct((slots, 128), F32),
        ),
        scratch_shapes=[
            pltpu.VMEM((requests, 128), F32),
            pltpu.VMEM((tiles * KDIM, 256), BF16),
            pltpu.VMEM((tiles * NF, 128), F32),
            pltpu.VMEM((tiles * 2, 128), F32),
        ],
        compiler_params=params(40, 1),
        cost_estimate=cost(4 * requests * slots * 256 * 2, tiles * KDIM * UNIT * 4),
    )(
        arrived,
        slot_row,
        slot_col,
        remap_w.reshape(tiles * KDIM, UNIT),
        incidence,
        sky_view,
        albedo,
    )
    returned = lax.all_to_all(
        outgoing.reshape(devices, CAP, 128), AXES, split_axis=0, concat_axis=0, tiled=True
    ).reshape(slots, 128)

    mixed = mix(mixing, atm_state, 0, 0, 2 * LEV)
    ocean = pl.pallas_call(
        ocean_kernel,
        out_shape=jax.ShapeDtypeStruct((NF, columns), F32),
        compiler_params=params(16),
        cost_estimate=cost(columns * 100, columns * 64, columns * 4),
    )(forcing, ocean_mask.reshape(1, columns))

    rows = 1024
    atm_out, col_flux = pl.pallas_call(
        finish_kernel,
        grid=(columns // rows,),
        in_specs=[
            whole(slots, 128),
            whole(devices, 128),
            whole(NF, columns),
            pl.BlockSpec((rows, 256), lambda i: (i, 0)),
            pl.BlockSpec(memory_space=pl.ANY),
        ],
        out_specs=(
            pl.BlockSpec((rows, 256), lambda i: (i, 0)),
            whole(NF, columns),
        ),
        out_shape=(
            jax.ShapeDtypeStruct((columns, NV * LEV), BF16),
            jax.ShapeDtypeStruct((NF, columns), F32),
        ),
        input_output_aliases={4: 0},
        compiler_params=params(16, 1),
    )(returned, incoming, ocean, mixed, kept)
    return (atm_out, land_temp, col_flux)


def solution(mesh):
    return jax.shard_map(
        on_device,
        mesh=mesh,
        in_specs=(
            P(AXES, None),
            P(),
            P(),
            P(None, AXES),
            P(AXES),
            P(AXES, None),
            P(AXES, None),
            P(AXES, None, None),
            P(AXES, None),
            P(AXES, None),
            P(AXES, None),
            P(AXES, None),
            P(AXES),
            P(AXES),
        ),
        out_specs=(P(AXES, None), P(AXES, None), P(None, AXES)),
        check_vma=False,
    )
```

profile of v0, /device:TPU:1, one launch (start us, length us, event | category | flops | bytes accessed | tf_op | source)
XLA Modules:
  0.0 97.3 jit_solution(3468998622033562288)
XLA Ops:
  0.7 0.7 copy-done.5
  1.4 0.7 copy-done.6
  2.0 1.2 %shard_map.157 = (s32[128,128]{1,0:T(8,128)}, s32[4,256]{1,0:T(4,128)S(1)}, s32[256,8]{1,0:T(8,128)S(1)}) custom-call(s32[4,256]{1,0:T(4,128)S(1)} %bitcast.18, s32[4,256]{1,0:T(4,128)S(1)} %bitcast.19), custom_call_target="tpu_custom_call" | custom-call | tf_op jit(solution)/shard_map/pallas_call | solution.py:425
  3.2 11.5 %all-to-all-start = ((s32[128,1,128]{2,1,0:T(1,128)}), s32[128,1,128]{2,1,0:T(1,128)S(1)}, u32[]{:S(2)}, u32[]{:S(2)}) async-start(s32[128,1,128]{2,1,0:T(1,128)} %bitcast.3), calls=%async_computation | async-start | bytes 131072 | tf_op jit(solution)/shard_map/all_to_all | solution.py:434
  14.7 0.0 copy-start
  14.7 2.2 %copy-done = bf16[4096,512]{1,0:T(8,128)(2,1)S(1)} copy-done((bf16[4096,512]{1,0:T(8,128)(2,1)S(1)}, bf16[4096,512]{1,0:T(8,128)(2,1)}, u32[]{:S(2)}) %copy-start) | copy-done | bytes 4194328
  16.9 0.8 copy-done.3
  17.7 0.7 copy-done.7
  18.4 3.9 %shard_map.158 = (f32[8,4096]{1,0:T(8,128)S(1)}, bf16[256,256]{1,0:T(8,128)(2,1)S(1)}) custom-call(f32[1,128]{1,0:T(1,128)S(1)} %bitcast.20, bf16[4096,512]{1,0:T(8,128)(2,1)S(1)} %copy-done, f32[4,4096]{1,0:T(4,128)S(1)} %copy-done.3), custom_call_target="tpu_custom_call" | custom-call | flops 134217728 | bytes 4194304 | tf_op jit(solution)/shard_map/pallas_call | solution.py:437
  22.3 1.7 %all-to-all-done = s32[128,1,128]{2,1,0:T(1,128)S(1)} async-done(((s32[128,1,128]{2,1,0:T(1,128)}), s32[128,1,128]{2,1,0:T(1,128)S(1)}, u32[]{:S(2)}, u32[]{:S(2)}) %all-to-all-start) | async-done | bytes 65568 | tf_op jit(solution)/shard_map/all_to_all | solution.py:434
  24.0 1.6 %shard_map.159 = f32[2048,128]{1,0:T(8,128)} custom-call(s32[128,128]{1,0:T(8,128)S(1)} %bitcast.15, bf16[256,256]{1,0:T(8,128)(2,1)S(1)} %get-tuple-element.13.blocks_ref), custom_call_target="tpu_custom_call" | custom-call | flops 268435456 | bytes 1048576 | tf_op jit(solution)/shard_map/pallas_call | solution.py:457
  25.6 8.1 %all-to-all-start.1 = ((f32[128,16,128]{2,1,0:T(8,128)}), f32[128,16,128]{2,1,0:T(8,128)S(1)}, u32[]{:S(2)}, u32[]{:S(2)}) async-start(f32[128,16,128]{2,1,0:T(8,128)} %bitcast.6), calls=%async_computation.1 | async-start | bytes 2097152 | tf_op jit(solution)/shard_map/all_to_all | solution.py:463
  33.8 1.0 maximum_divide_fusion.incidence_ref
  34.7 18.1 %all-to-all-done.1 = f32[128,16,128]{2,1,0:T(8,128)S(1)} async-done(((f32[128,16,128]{2,1,0:T(8,128)}), f32[128,16,128]{2,1,0:T(8,128)S(1)}, u32[]{:S(2)}, u32[]{:S(2)}) %all-to-all-start.1) | async-done | bytes 1048608 | tf_op jit(solution)/shard_map/all_to_all | solution.py:463
  52.9 3.4 %copy-done.8 = f32[256,64,128]{2,1,0:T(8,128)S(1)} copy-done((f32[256,64,128]{2,1,0:T(8,128)S(1)}, f32[256,64,128]{2,1,0:T(8,128)}, u32[]{:S(2)}) %copy-start.8) | copy-done | bytes 8388632
  56.3 12.9 %shard_map.160 = (f32[256,128]{1,0:T(8,128)}, f32[2048,128]{1,0:T(8,128)}) custom-call(f32[2048,128]{1,0:T(8,128)S(1)} %bitcast.14, s32[4,256]{1,0:T(4,128)S(1)} %get-tuple-element.14.row_ref, s32[256,8]{1,0:T(8,128)S(1)} %get-tuple-element.15.col_ref, f32[16384,128]{1,0:T(8,128)S(1)} %bitcast.21, f32[256,128]{1,0:T(8,128)S(1)} %maximum_divide_fusion.incidence_ref, ...), custom_call_target="tpu_custom_call" | custom-call | flops 4294967296 | bytes 8388608 | tf_op jit(solution)/shard_map/pallas_call | solution.py:482
  69.2 4.6 %all-to-all-start.2 = ((f32[128,16,128]{2,1,0:T(8,128)}), f32[128,16,128]{2,1,0:T(8,128)S(1)}, u32[]{:S(2)}, u32[]{:S(2)}) async-start(f32[128,16,128]{2,1,0:T(8,128)} %bitcast.9), calls=%async_computation.2 | async-start | bytes 2097152 | tf_op jit(solution)/shard_map/all_to_all | solution.py:516
  73.8 0.1 shard_map.161.ocean_ref
  73.9 0.0 copy-start.1
  73.9 2.2 %copy-done.1 = bf16[4096,512]{1,0:T(8,128)(2,1)S(1)} copy-done((bf16[4096,512]{1,0:T(8,128)(2,1)S(1)}, bf16[4096,512]{1,0:T(8,128)(2,1)}, u32[]{:S(2)}) %copy-start.1) | copy-done | bytes 4194328
  76.1 7.6 %shard_map.162.mixed_ref = bf16[4096,256]{1,0:T(8,128)(2,1)S(1)} custom-call(bf16[4,128,128]{2,1,0:T(8,128)(2,1)S(1)} %copy-done.2, bf16[4096,512]{1,0:T(8,128)(2,1)S(1)} %copy-done.1), custom_call_target="tpu_custom_call" | custom-call | flops 2147483648 | bytes 4194304 | tf_op jit(solution)/shard_map/pallas_call | solution.py:388
  83.7 8.3 %shard_map.163.kept_ref = bf16[4096,512]{1,0:T(8,128)(2,1)} custom-call(bf16[4,128,128]{2,1,0:T(8,128)(2,1)S(1)} %copy-done.2, bf16[4096,512]{1,0:T(8,128)(2,1)S(1)} %copy-done.1), custom_call_target="tpu_custom_call" | custom-call | flops 2147483648 | bytes 4194304 | tf_op jit(solution)/shard_map/pallas_call | solution.py:388
  92.0 1.1 %all-to-all-done.2 = f32[128,16,128]{2,1,0:T(8,128)S(1)} async-done(((f32[128,16,128]{2,1,0:T(8,128)}), f32[128,16,128]{2,1,0:T(8,128)S(1)}, u32[]{:S(2)}, u32[]{:S(2)}) %all-to-all-start.2) | async-done | bytes 1048608 | tf_op jit(solution)/shard_map/all_to_all | solution.py:516
  93.1 4.2 %shard_map.164 = (bf16[4096,512]{1,0:T(8,128)(2,1)}, f32[8,4096]{1,0:T(8,128)}) custom-call(f32[2048,128]{1,0:T(8,128)S(1)} %bitcast.13, s32[128,128]{1,0:T(8,128)S(1)} %bitcast.16, f32[8,4096]{1,0:T(8,128)S(1)} %shard_map.161.ocean_ref, bf16[4096,256]{1,0:T(8,128)(2,1)S(1)} %shard_map.162.mixed_ref, ...), custom_call_target="tpu_custom_call", output_to_operand_aliasing={{0}: (4, {})} | custom-call | tf_op jit(solution)/shard_map/pallas_call | solution.py:529
  (22 shorter events, 0.0 us)
Async XLA Ops:
  0.6 33.1 %copy-start.13 = (f32[256]{0:T(256)S(1)}, f32[256]{0:T(256)}, u32[]{:S(2)}) copy-start(f32[256]{0:T(256)} %param.26) | copy-start | bytes 3076
  0.6 33.1 %copy-start.14 = (f32[256]{0:T(256)S(1)}, f32[256]{0:T(256)}, u32[]{:S(2)}) copy-start(f32[256]{0:T(256)} %param.27) | copy-start | bytes 3076
  0.7 0.7 copy-start.5
  1.4 0.7 copy-start.6
  2.0 50.8 %copy-start.9 = (f32[256,128]{1,0:T(8,128)S(1)}, f32[256,128]{1,0:T(8,128)}, u32[]{:S(2)}) copy-start(f32[256,128]{1,0:T(8,128)} %sky_ref.1) | copy-start | bytes 393220
  3.2 20.8 %all-to-all-start = ((s32[128,1,128]{2,1,0:T(1,128)}), s32[128,1,128]{2,1,0:T(1,128)S(1)}, u32[]{:S(2)}, u32[]{:S(2)}) async-start(s32[128,1,128]{2,1,0:T(1,128)} %bitcast.3), calls=%async_computation | async-start | bytes 131072 | tf_op jit(solution)/shard_map/all_to_all | solution.py:434
  14.7 2.2 %copy-start = (bf16[4096,512]{1,0:T(8,128)(2,1)S(1)}, bf16[4096,512]{1,0:T(8,128)(2,1)}, u32[]{:S(2)}) copy-start(bf16[4096,512]{1,0:T(8,128)(2,1)} %state_ref.5) | copy-start | bytes 12582916
  16.9 0.8 copy-start.3
  17.7 0.7 copy-start.7
  18.4 15.4 %copy-start.11 = (s32[256,128]{1,0:T(8,128)S(1)}, s32[256,128]{1,0:T(8,128)}, u32[]{:S(2)}) copy-start(s32[256,128]{1,0:T(8,128)} %param.23) | copy-start | bytes 393220
  18.4 15.4 %copy-start.12 = (s32[256,128]{1,0:T(8,128)S(1)}, s32[256,128]{1,0:T(8,128)}, u32[]{:S(2)}) copy-start(s32[256,128]{1,0:T(8,128)} %param.22) | copy-start | bytes 393220
  18.4 34.5 %copy-start.10 = (f32[256,128]{1,0:T(8,128)S(1)}, f32[256,128]{1,0:T(8,128)}, u32[]{:S(2)}) copy-start(f32[256,128]{1,0:T(8,128)} %albedo_ref.1) | copy-start | bytes 393220
  25.6 27.3 %all-to-all-start.1 = ((f32[128,16,128]{2,1,0:T(8,128)}), f32[128,16,128]{2,1,0:T(8,128)S(1)}, u32[]{:S(2)}, u32[]{:S(2)}) async-start(f32[128,16,128]{2,1,0:T(8,128)} %bitcast.6), calls=%async_computation.1 | async-start | bytes 2097152 | tf_op jit(solution)/shard_map/all_to_all | solution.py:463
  52.9 3.4 %copy-start.8 = (f32[256,64,128]{2,1,0:T(8,128)S(1)}, f32[256,64,128]{2,1,0:T(8,128)}, u32[]{:S(2)}) copy-start(f32[256,64,128]{2,1,0:T(8,128)} %param.21) | copy-start | bytes 25165828
  56.3 17.5 %copy-start.4 = (s32[4096]{0:T(1024)S(1)}, s32[4096]{0:T(1024)}, u32[]{:S(2)}) copy-start(s32[4096]{0:T(1024)} %param.18) | copy-start | bytes 49156
  56.3 17.6 %copy-start.2 = (bf16[4,128,128]{2,1,0:T(8,128)(2,1)S(1)}, bf16[4,128,128]{2,1,0:T(8,128)(2,1)}, u32[]{:S(2)}) copy-start(bf16[4,128,128]{2,1,0:T(8,128)(2,1)} %mixing_ref.3) | copy-start | bytes 393220
  69.2 23.9 %all-to-all-start.2 = ((f32[128,16,128]{2,1,0:T(8,128)}), f32[128,16,128]{2,1,0:T(8,128)S(1)}, u32[]{:S(2)}, u32[]{:S(2)}) async-start(f32[128,16,128]{2,1,0:T(8,128)} %bitcast.9), calls=%async_computation.2 | async-start | bytes 2097152 | tf_op jit(solution)/shard_map/all_to_all | solution.py:516
  73.9 2.2 %copy-start.1 = (bf16[4096,512]{1,0:T(8,128)(2,1)S(1)}, bf16[4096,512]{1,0:T(8,128)(2,1)}, u32[]{:S(2)}) copy-start(bf16[4096,512]{1,0:T(8,128)(2,1)} %state_ref.5) | copy-start | bytes 12582916
where the time goes:
time: 97.8 us; the launch traced here: 97.3 us
  Pallas kernels  39.8 us (41%)
  starting transfers between devices  24.2 us (25%)
  waiting for transfers between devices  20.9 us (21%)
  local copies, waits for them, and re-layouts  10.7 us (11%)
    all_to_all x1, waiting for transfers between devices, on_device(): lax.all_to_all(reply.reshape(devices, CAP, 128), AXES, split_axis=0, conc...  18.1 us
    pallas_call x2, Pallas kernels, mix(): pl.pallas_call(mix_kernel, grid=(columns // rows,), in_specs=[pl.BlockSpe...  15.9 us
    pallas_call x1, Pallas kernels, on_device(): pl.pallas_call(land_kernel, grid=(tiles // step_tiles,), in_specs=[whole(...  12.9 us
    all_to_all x1, starting transfers between devices, on_device(): lax.all_to_all(wanted, AXES, split_axis=0, concat_axis=0, tiled=True)  11.5 us
    unnamed x30, local copies, waits for them, and re-layouts  10.7 us
    all_to_all x1, starting transfers between devices, on_device(): lax.all_to_all(reply.reshape(devices, CAP, 128), AXES, split_axis=0, conc...  8.08 us
    all_to_all x1, starting transfers between devices, on_device(): lax.all_to_all(outgoing.reshape(devices, CAP, 128), AXES, split_axis=0, c...  4.61 us
    pallas_call x1, Pallas kernels, on_device(): pl.pallas_call(finish_kernel, grid=(columns // rows,), in_specs=[whole(sl...  4.18 us
  transfers between devices with their start and end apart: 3, of which 3 were waited for; matrix products, arithmetic and copies ran while one was open for 1% of the time, Pallas kernels for 20%

commit v1 on v0

v1 whole, which is shorter than its diff:
```python
import functools
import math

import jax
import jax.numpy as jnp
from jax import lax
from jax.experimental import pallas as pl
from jax.experimental.pallas import tpu as pltpu
from jax.sharding import PartitionSpec as P

GLL = 16
LEV = 128
NV = 4
NF = 8
SUB = 4
NEWTON = 2
NASPECT = 8
CAP = 16
UNIT = 128
REF = 4
KDIM = REF * GLL
AXES = ("sect", "lane")

F32 = jnp.float32
BF16 = jnp.bfloat16
I32 = jnp.int32
MIB = 1 << 20


def iota(shape, axis):
    return lax.broadcasted_iota(I32, shape, axis)


def matmul(left, right):
    return jnp.dot(left, right, preferred_element_type=F32)


def matmul_nt(left, right):
    return lax.dot_general(left, right, (((1,), (1,)), ((), ())), preferred_element_type=F32)


def flag(condition):
    return jnp.where(condition, 1.0, 0.0).astype(BF16)


def high_low(values):
    high = values.astype(BF16).astype(F32)
    return high, values - high


def pair(values):
    high, low = high_low(values)
    return jnp.concatenate([high.astype(BF16), low.astype(BF16)], axis=1)


def fold(values):
    half = values.shape[1] // 2
    return values[:, :half] + values[:, half:]


def block_swap(values):
    cube = values.reshape(values.shape[0] // 8, 8, 128)
    rows, lanes = iota(cube.shape, 1), iota(cube.shape, 2)
    for step in range(3):
        reach = 1 << step
        row_bit, chunk_bit = (rows >> step) & 1, (lanes >> (4 + step)) & 1
        up = pltpu.roll(pltpu.roll(cube, 8 - reach, 1), 16 * reach, 2)
        if reach == 4:
            moved = up
        else:
            down = pltpu.roll(pltpu.roll(cube, reach, 1), 128 - 16 * reach, 2)
            moved = jnp.where(chunk_bit == 1, up, down)
        cube = jnp.where(row_bit == chunk_bit, cube, moved)
    return cube.reshape(values.shape)


def drivers(fields):
    air_temp = 1.0 + 0.05 * jnp.tanh(fields[0])
    air_humid = 0.02 / (1.0 + jnp.exp(-fields[1]))
    wind_speed = jnp.sqrt(1.0 + fields[2] * fields[2] + fields[3] * fields[3])
    return (
        air_temp,
        air_humid,
        wind_speed,
        1.5 * fields[4],
        0.5 * fields[5],
        0.6 + 0.3 * fields[6],
        fields[7],
    )


def flux_list(surface, fields, driven, absorbed, reflected, wetness):
    air_temp, air_humid, wind_speed = driven[:3]
    heat_coef = 0.1 * wind_speed
    vapor_coef = 0.25 * wind_speed * wetness
    saturation = 0.02 * jnp.exp(17.0 * (surface - 1.0))
    sensible = heat_coef * (surface - air_temp)
    latent = vapor_coef * (saturation - air_humid)
    square = surface * surface
    upward = 0.95 * (square * square)
    drag = 0.05 * wind_speed
    return [
        sensible,
        latent,
        upward,
        reflected,
        drag * fields[2],
        drag * fields[3],
        0.4 * latent,
        absorbed - upward - sensible - latent,
    ]


def start_copies(source, target, sems, parts):
    rows = target.shape[0] // parts
    copies = []
    for part in range(parts):
        span = pl.ds(part * rows, rows)
        copy = pltpu.make_async_copy(source.at[span, :], target.at[span, :], sems.at[part])
        copy.start()
        copies.append(copy)
    return copies


def route_kernel(src_ref, elem_ref, want_ref, row_ref, col_ref):
    devices, tiles = want_ref.shape[0], src_ref.shape[1]
    owner = iota((devices, tiles), 0)
    slot = iota((128, tiles), 0)
    earlier = flag(iota((tiles, tiles), 0) < iota((tiles, tiles), 1))
    base = jnp.zeros((devices, 1), F32)
    wanted = jnp.zeros((devices, 128), F32)
    places = []
    for ref in range(REF):
        source = src_ref[ref : ref + 1, :]
        hit = owner == source
        onehot = flag(hit)
        before = matmul(onehot, earlier) + base
        rank = jnp.sum(jnp.where(hit, before, 0.0), axis=0, keepdims=True)
        base = base + jnp.sum(jnp.where(hit, 1.0, 0.0), axis=1, keepdims=True)
        rank = rank.astype(I32)
        value = (elem_ref[ref : ref + 1, :] + 1).astype(F32)
        table = jnp.where(slot == rank, value, 0.0).astype(BF16)
        wanted = wanted + matmul_nt(onehot, table)
        places.append(source * CAP + rank)
    want_ref[...] = wanted.astype(I32) - 1
    for ref in range(REF):
        row_ref[ref : ref + 1, :] = places[ref]
    stacked = jnp.concatenate(places + places, axis=0).astype(F32)
    col_ref[...] = jnp.transpose(stacked).astype(I32)


def forcing_kernel(
    profile_ref,
    state_ref,
    radiation_ref,
    forcing_ref,
    blocks_ref,
    held_ref,
    sems,
):
    parts = sems.shape[0]
    copies = start_copies(state_ref, held_ref, sems, parts)
    profile = profile_ref[...]
    first = profile.astype(BF16).astype(F32)
    second = (profile - first).astype(BF16).astype(F32)
    third = profile - first - second
    rows = iota((32, LEV), 0)
    piece = jnp.where(rows < 8, first, jnp.where(rows < 16, second, jnp.where(rows < 24, third, 0.0)))
    spread = jnp.concatenate(
        [jnp.where((rows & 7) == variable, piece, 0.0) for variable in range(NV)], axis=1
    ).astype(BF16)
    size = held_ref.shape[0] // parts
    pieces = []
    for part in range(parts):
        copies[part].wait()
        columns = slice(part * size, part * size + size)
        sums = matmul_nt(spread, held_ref[columns, :])
        means = sums[0:8] + sums[8:16] + sums[16:24]
        forcing = jnp.concatenate([means[0:NV], radiation_ref[:, columns]], axis=0)
        forcing_ref[:, columns] = forcing
        pieces += [forcing[:, start : start + 128] for start in range(0, size, 128)]
    blocks_ref[...] = pair(block_swap(jnp.concatenate(pieces, axis=0)))


def reply_kernel(incoming_ref, blocks_ref, reply_ref):
    devices, elements = incoming_ref.shape[0], blocks_ref.shape[0]
    element = iota((devices, elements), 1)
    blocks = blocks_ref[...]
    incoming = incoming_ref[...]
    for slot in range(CAP):
        select = flag(element == incoming[:, slot : slot + 1])
        reply_ref[pl.ds(slot, devices, stride=CAP), :] = fold(matmul(select, blocks))


def prepare_kernel(w_ref, both_ref, inverse_ref):
    rows = w_ref.shape[0]
    part = 1024
    for start in range(0, rows, part):
        weights = w_ref[start : start + part, :]
        both_ref[start : start + part, :] = pair(weights)
        total = jnp.sum(weights.reshape(part // KDIM, KDIM, UNIT), axis=1)
        inverse_ref[start // KDIM : (start + part) // KDIM, :] = 1.0 / total


def mix_rows(mixing_ref, held_ref, size, done):
    zero = jnp.zeros((LEV, LEV), BF16)
    operator = jnp.concatenate(
        [
            jnp.concatenate([mixing_ref[0], zero], axis=1),
            jnp.concatenate([zero, mixing_ref[1]], axis=1),
        ],
        axis=0,
    )

    def work(part, carry):
        done(part, None)
        span = pl.ds(pl.multiple_of(part * size, size), size)
        state = held_ref[span, :]
        for iteration in range(SUB):
            update = matmul(state, operator)
            state = (state.astype(F32) + 0.25 * jnp.tanh(update)).astype(BF16)
        done(part, state)
        return carry

    lax.fori_loop(0, held_ref.shape[0] // size, work, 0)


def mix_kernel(half, out_half, mixing_ref, state_ref, mixed_ref, held_ref, into, out):
    parts = into.shape[0]
    size = held_ref.shape[0] // parts
    lanes = pl.ds(half * 256, 256)

    def copy_in(part):
        span = pl.ds(pl.multiple_of(part * size, size), size)
        return pltpu.make_async_copy(state_ref.at[span, lanes], held_ref.at[span, :], into.at[part])

    def copy_out(part):
        span = pl.ds(pl.multiple_of(part * size, size), size)
        return pltpu.make_async_copy(
            held_ref.at[span, :], mixed_ref.at[span, pl.ds(out_half * 256, 256)], out.at[part]
        )

    for part in range(parts):
        copy_in(part).start()

    def done(part, state):
        if state is None:
            copy_in(part).wait()
            return
        span = pl.ds(pl.multiple_of(part * size, size), size)
        if out_half is None:
            mixed_ref[span, :] = state
        else:
            held_ref[span, :] = state
            copy_out(part).start()

    mix_rows(mixing_ref, held_ref, size, done)
    if out_half is not None:
        for part in range(parts):
            copy_out(part).wait()


def ocean_kernel(forcing_ref, mask_ref, ocean_ref):
    fields = [forcing_ref[index : index + 1, :] for index in range(NF)]
    driven = drivers(fields)
    shortwave = driven[3] + driven[4]
    absorbed = 0.94 * shortwave + 0.95 * driven[5]
    one = jnp.ones_like(fields[0])
    fluxes = flux_list(one, fields, driven, absorbed, 0.06 * shortwave, one)
    mask = mask_ref[...].astype(F32)
    for index in range(NF):
        ocean_ref[index : index + 1, :] = mask * fluxes[index]


def land_kernel(
    arrived_ref,
    row_ref,
    col_ref,
    both_ref,
    inverse_ref,
    incidence_ref,
    sky_ref,
    albedo_ref,
    temp_ref,
    outgoing_ref,
    need_ref,
    raw_ref,
    held_ref,
    sems,
):
    slots = arrived_ref.shape[0]
    tiles = row_ref.shape[1]
    parts = sems.shape[0]
    copies = start_copies(both_ref, held_ref, sems, parts)
    arrived = pair(arrived_ref[...])
    slot = iota((tiles, slots), 1)
    for ref in range(REF):
        pick = flag(slot == col_ref[:, ref : ref + 1])
        need_ref[pl.ds(ref, tiles, stride=REF), :] = fold(matmul(pick, arrived))
    need_ref[...] = block_swap(need_ref[...])

    left = iota((8, 128), 1) < KDIM
    zero = jnp.zeros((8, 128), F32)

    def take(group, carry):
        weights = held_ref[pl.ds(pl.multiple_of(group * 256, 256), 256), :]
        need = need_ref[pl.ds(pl.multiple_of(group * 16, 16), 16), :]
        rows = []
        for part in high_low(need):
            for half in range(2):
                block = part[half * 8 : half * 8 + 8]
                for masked in (jnp.where(left, block, 0.0), jnp.where(left, 0.0, block)):
                    rows.append(
                        jnp.concatenate([masked, zero] if half == 0 else [zero, masked], axis=1)
                    )
        product = fold(matmul(jnp.concatenate(rows, axis=0).astype(BF16), weights))
        raw_ref[pl.ds(pl.multiple_of(group * 32, 32), 32), :] = product[0:32] + product[32:64]
        return carry

    size = tiles // 4 // parts
    for part in range(parts):
        copies[part].wait()
        lax.fori_loop(part * size, (part + 1) * size, take, 0, unroll=8)

    inverse = inverse_ref[...]
    fields = [raw_ref[pl.ds(index, tiles, stride=NF), :] * inverse for index in range(NF)]
    driven = drivers(fields)
    air_temp, air_humid, wind_speed, direct_sw, diffuse_sw, longwave, wetness = driven
    sky, albedo = sky_ref[...], albedo_ref[...]
    shortwave = direct_sw * incidence_ref[...] + diffuse_sw * sky
    absorbed = (1.0 - albedo) * shortwave + 0.95 * longwave * sky
    heat_coef = 0.1 * wind_speed
    vapor_coef = 0.25 * wind_speed * wetness
    surface = air_temp
    for iteration in range(NEWTON):
        saturation = 0.02 * jnp.exp(17.0 * (surface - 1.0))
        square = surface * surface
        imbalance = (
            absorbed
            - 0.95 * (square * square)
            - heat_coef * (surface - air_temp)
            - vapor_coef * (saturation - air_humid)
        )
        derivative = -3.8 * (square * surface) - heat_coef - 17.0 * vapor_coef * saturation
        surface = surface - imbalance / derivative
    temp_ref[...] = surface
    fluxes = flux_list(surface, fields, driven, absorbed, albedo * shortwave, wetness)
    for index in range(NF):
        raw_ref[pl.ds(index, tiles, stride=NF), :] = fluxes[index] * inverse

    def give(group, carry):
        flux = raw_ref[pl.ds(pl.multiple_of(group * 32, 32), 32), :]
        high, low = high_low(flux)
        stacked = jnp.concatenate([high, low], axis=0).astype(BF16)
        stacked = jnp.concatenate([stacked, stacked], axis=1)
        weights = held_ref[pl.ds(pl.multiple_of(group * 256, 256), 256), :]
        product = matmul_nt(stacked, weights)
        product = product[0:32] + product[32:64]
        need_ref[pl.ds(pl.multiple_of(group * 16, 16), 16), :] = jnp.concatenate(
            [
                jnp.where(left, product[0:8, 0:128], product[8:16, 0:128]),
                jnp.where(left, product[16:24, 128:256], product[24:32, 128:256]),
            ],
            axis=0,
        )
        return carry

    lax.fori_loop(0, tiles // 4, give, 0, unroll=16)
    need_ref[...] = block_swap(need_ref[...])
    given = jnp.concatenate(
        [pair(need_ref[pl.ds(ref, tiles, stride=REF), :]) for ref in range(REF)], axis=0
    )
    size = 256

    def place(index, carry):
        start = pl.multiple_of(index * size, size)
        spot = iota((size, tiles), 0) + start
        pick = jnp.concatenate(
            [flag(spot == row_ref[ref : ref + 1, :]) for ref in range(REF)], axis=1
        )
        outgoing_ref[pl.ds(start, size), :] = fold(matmul(pick, given))
        return carry

    lax.fori_loop(0, slots // size, place, 0, unroll=4)


def finish_kernel(
    returned_ref, incoming_ref, ocean_ref, mixed_ref, kept_ref, out_ref, flux_ref, held_ref, sems
):
    del kept_ref
    devices = incoming_ref.shape[0]
    elements = flux_ref.shape[1] // GLL
    incoming = jnp.transpose(incoming_ref[...].astype(F32)).astype(I32)
    element = iota((elements, devices), 0)
    part = jnp.zeros((elements, 256), F32)
    for slot in range(0, CAP, 2):
        select = jnp.concatenate(
            [flag(element == incoming[slot + extra : slot + extra + 1, :]) for extra in range(2)],
            axis=1,
        )
        values = jnp.concatenate(
            [pair(returned_ref[pl.ds(slot + extra, devices, stride=CAP), :]) for extra in range(2)],
            axis=0,
        )
        part = part + matmul(select, values)
    swapped = block_swap(fold(part))
    parts = sems.shape[0]
    size = held_ref.shape[0] // parts
    lane = iota((128, 128), 1)
    copies = []
    for index in range(parts):
        for start in range(index * size, index * size + size, 128):
            columns = slice(start, start + 128)
            flux = swapped[start // 16 : start // 16 + 8] + ocean_ref[:, columns]
            flux_ref[:, columns] = flux
            turned = jnp.transpose(flux)
            for half, row in ((0, 0), (1, 6)):
                lanes = slice(half * 128, half * 128 + 128)
                added = jnp.where(lane == 0, 0.1 * turned[:, row : row + 1], 0.0)
                state = mixed_ref[columns, lanes].astype(F32)
                held_ref[columns, lanes] = (state + added).astype(BF16)
        span = pl.ds(index * size, size)
        copy = pltpu.make_async_copy(
            held_ref.at[span, :], out_ref.at[span, pl.ds(0, 256)], sems.at[index]
        )
        copy.start()
        copies.append(copy)
    for copy in copies:
        copy.wait()


def whole(*shape):
    return pl.BlockSpec(shape, lambda *_: (0,) * len(shape))


def params(mebibytes, axes=0):
    return pltpu.CompilerParams(
        vmem_limit_bytes=mebibytes * MIB,
        dimension_semantics=("arbitrary",) * axes if axes else None,
    )


def cost(flops, moved, hard=0):
    return pl.CostEstimate(flops=int(flops), bytes_accessed=int(moved), transcendentals=int(hard))


def mix(mixing, atm_state, half, out_half):
    columns = atm_state.shape[0]
    parts = 4
    apart = out_half is None
    return pl.pallas_call(
        functools.partial(mix_kernel, half, out_half),
        grid=(1,),
        in_specs=[
            pl.BlockSpec((2, LEV, LEV), lambda i: (half, 0, 0)),
            pl.BlockSpec(memory_space=pltpu.HBM),
        ],
        out_specs=whole(columns, 256) if apart else pl.BlockSpec(memory_space=pltpu.HBM),
        out_shape=jax.ShapeDtypeStruct((columns, 256 if apart else NV * LEV), BF16),
        scratch_shapes=[
            pltpu.VMEM((columns, 256), BF16),
            pltpu.SemaphoreType.DMA((parts,)),
            pltpu.SemaphoreType.DMA((parts,)),
        ],
        compiler_params=params(16, 1),
        cost_estimate=cost(columns * 256 * 256 * 2 * SUB, columns * 256 * 4, columns * 256 * SUB),
    )(mixing, atm_state)


def on_device(
    atm_state,
    profile,
    mixing,
    radiation,
    ocean_mask,
    tile_src,
    tile_elem,
    remap_w,
    slope_class,
    aspect_class,
    sky_view,
    albedo,
    sun_cos,
    sun_azimuth,
):
    devices = lax.axis_size("sect") * lax.axis_size("lane")
    columns = atm_state.shape[0]
    elements = columns // GLL
    tiles = tile_src.shape[0]
    slots = devices * CAP
    requests = tiles * REF

    wanted, slot_row, slot_col = pl.pallas_call(
        route_kernel,
        out_shape=(
            jax.ShapeDtypeStruct((devices, 128), I32),
            jax.ShapeDtypeStruct((REF, tiles), I32),
            jax.ShapeDtypeStruct((tiles, 2 * REF), I32),
        ),
        compiler_params=params(60),
    )(tile_src.T, tile_elem.T)
    wanted, atm_state = lax.optimization_barrier((wanted, atm_state))
    incoming = lax.all_to_all(wanted, AXES, split_axis=0, concat_axis=0, tiled=True)

    parts = 4
    forcing, blocks = pl.pallas_call(
        forcing_kernel,
        grid=(1,),
        in_specs=[
            whole(1, LEV),
            pl.BlockSpec(memory_space=pltpu.HBM),
            whole(4, columns),
        ],
        out_specs=(whole(NF, columns), whole(elements, 256)),
        out_shape=(
            jax.ShapeDtypeStruct((NF, columns), F32),
            jax.ShapeDtypeStruct((elements, 256), BF16),
        ),
        scratch_shapes=[
            pltpu.VMEM((columns, NV * LEV), BF16),
            pltpu.SemaphoreType.DMA((parts,)),
        ],
        compiler_params=params(50, 1),
        cost_estimate=cost(columns * 512 * 32 * 2, columns * 1024),
    )(profile.reshape(1, LEV), atm_state, radiation)
    incoming, forcing, blocks = lax.optimization_barrier((incoming, forcing, blocks))

    reply = pl.pallas_call(
        reply_kernel,
        out_shape=jax.ShapeDtypeStruct((slots, 128), F32),
        compiler_params=params(16),
        cost_estimate=cost(slots * 256 * 256 * 2, slots * 512),
    )(incoming, blocks)
    reply, atm_state, remap_w, slope_class, sun_cos = lax.optimization_barrier(
        (reply, atm_state, remap_w, slope_class, sun_cos)
    )
    arrived = lax.all_to_all(
        reply.reshape(devices, CAP, 128), AXES, split_axis=0, concat_axis=0, tiled=True
    ).reshape(slots, 128)

    kept = mix(mixing, atm_state, 1, 1)
    cosine = sun_cos[:, None]
    sine = jnp.sqrt(1.0 - cosine * cosine)
    slope_angle = slope_class.astype(F32) * 0.1
    aspect_angle = aspect_class.astype(F32) * (2.0 * math.pi / NASPECT)
    incidence = (
        jnp.maximum(
            0.0,
            jnp.cos(slope_angle) * cosine
            + jnp.sin(slope_angle) * sine * jnp.cos(sun_azimuth[:, None] - aspect_angle),
        )
        / cosine
    )
    remap_w, kept, incidence = lax.optimization_barrier((remap_w, kept, incidence))
    rows = 4096
    both, inverse = pl.pallas_call(
        prepare_kernel,
        grid=(tiles * KDIM // rows,),
        in_specs=[pl.BlockSpec((rows, UNIT), lambda i: (i, 0))],
        out_specs=(
            pl.BlockSpec((rows, 256), lambda i: (i, 0)),
            pl.BlockSpec((rows // KDIM, UNIT), lambda i: (i, 0)),
        ),
        out_shape=(
            jax.ShapeDtypeStruct((tiles * KDIM, 256), BF16),
            jax.ShapeDtypeStruct((tiles, UNIT), F32),
        ),
        compiler_params=params(20, 1),
        cost_estimate=cost(tiles * KDIM * UNIT * 8, tiles * KDIM * UNIT * 8),
    )(remap_w.reshape(tiles * KDIM, UNIT))
    arrived, kept, both, inverse, incidence = lax.optimization_barrier(
        (arrived, kept, both, inverse, incidence)
    )

    land_temp, outgoing = pl.pallas_call(
        land_kernel,
        grid=(1,),
        in_specs=[
            whole(slots, 128),
            whole(REF, tiles),
            whole(tiles, 2 * REF),
            pl.BlockSpec(memory_space=pltpu.HBM),
            whole(tiles, UNIT),
            whole(tiles, UNIT),
            whole(tiles, UNIT),
            whole(tiles, UNIT),
        ],
        out_specs=(whole(tiles, UNIT), whole(slots, 128)),
        out_shape=(
            jax.ShapeDtypeStruct((tiles, UNIT), F32),
            jax.ShapeDtypeStruct((slots, 128), F32),
        ),
        scratch_shapes=[
            pltpu.VMEM((requests, 128), F32),
            pltpu.VMEM((tiles * NF, 128), F32),
            pltpu.VMEM((tiles * KDIM, 256), BF16),
            pltpu.SemaphoreType.DMA((8,)),
        ],
        compiler_params=params(50, 1),
        cost_estimate=cost(4 * requests * slots * 256 * 2, tiles * KDIM * UNIT * 4),
    )(arrived, slot_row, slot_col, both, inverse, incidence, sky_view, albedo)
    outgoing, atm_state, forcing = lax.optimization_barrier((outgoing, atm_state, forcing))
    returned = lax.all_to_all(
        outgoing.reshape(devices, CAP, 128), AXES, split_axis=0, concat_axis=0, tiled=True
    ).reshape(slots, 128)

    mixed = mix(mixing, atm_state, 0, None)
    ocean = pl.pallas_call(
        ocean_kernel,
        out_shape=jax.ShapeDtypeStruct((NF, columns), F32),
        compiler_params=params(16),
        cost_estimate=cost(columns * 100, columns * 64, columns * 4),
    )(forcing, ocean_mask.reshape(1, columns))
    returned, mixed, ocean = lax.optimization_barrier((returned, mixed, ocean))

    atm_out, col_flux = pl.pallas_call(
        finish_kernel,
        grid=(1,),
        in_specs=[
            whole(slots, 128),
            whole(devices, 128),
            whole(NF, columns),
            whole(columns, 256),
            pl.BlockSpec(memory_space=pltpu.HBM),
        ],
        out_specs=(pl.BlockSpec(memory_space=pltpu.HBM), whole(NF, columns)),
        out_shape=(
            jax.ShapeDtypeStruct((columns, NV * LEV), BF16),
            jax.ShapeDtypeStruct((NF, columns), F32),
        ),
        scratch_shapes=[
            pltpu.VMEM((columns, 256), BF16),
            pltpu.SemaphoreType.DMA((parts,)),
        ],
        input_output_aliases={4: 0},
        compiler_params=params(16, 1),
    )(returned, incoming, ocean, mixed, kept)
    return (atm_out, land_temp, col_flux)


def solution(mesh):
    return jax.shard_map(
        on_device,
        mesh=mesh,
        in_specs=(
            P(AXES, None),
            P(),
            P(),
            P(None, AXES),
            P(AXES),
            P(AXES, None),
            P(AXES, None),
            P(AXES, None, None),
            P(AXES, None),
            P(AXES, None),
            P(AXES, None),
            P(AXES, None),
            P(AXES),
            P(AXES),
        ),
        out_specs=(P(AXES, None), P(AXES, None), P(None, AXES)),
        check_vma=False,
    )
```

time: 97.8 us -> 90.4 us (0.924)
  Pallas kernels: 39.8 us -> 32.9 us
  waiting for transfers between devices: 20.9 us -> 24.4 us
  starting transfers between devices: 24.2 us -> 21.4 us
  local copies, waits for them, and re-layouts: 10.7 us -> 9.18 us
    all_to_all x1, waiting for transfers between devices: 1.1 us -> 13.3 us  [on_device(): lax.all_to_all(outgoing.reshape(devices, CAP, 128), AXES, split_axis=0, c...]
    all_to_all x1, waiting for transfers between devices: 18.1 us -> 6.49 us  [on_device(): lax.all_to_all(reply.reshape(devices, CAP, 128), AXES, split_axis=0, conc...]
    pallas_call x5 -> x6, Pallas kernels: 37 us -> 29.3 us  [the longest x1 11.8 us: on_device(): pl.pallas_call(land_kernel, grid=(1,), in_specs=[whole(slots, 128), whole...]
    all_to_all x1, starting transfers between devices: 8.08 us -> 5.11 us  [on_device(): lax.all_to_all(reply.reshape(devices, CAP, 128), AXES, split_axis=0, conc...]
    all_to_all x1, waiting for transfers between devices: 1.7 us -> 4.66 us  [on_device(): lax.all_to_all(wanted, AXES, split_axis=0, concat_axis=0, tiled=True)]
    unnamed x30 -> x32, local copies, waits for them, and re-layouts: 10.7 us -> 9.18 us
  transfers between devices with their start and end apart: 3 -> 3, of which waited for: 3 -> 3; matrix products, arithmetic and copies ran while one was open for 1% -> 1% of each run, Pallas kernels for 20% -> 15%
where the time goes in v1:
time: 90.4 us; the launch traced here: 90 us
  Pallas kernels  32.9 us (36%)
  waiting for transfers between devices  24.4 us (27%)
  starting transfers between devices  21.4 us (24%)
  local copies, waits for them, and re-layouts  9.18 us (10%)
  between operations  1.03 us (1%)
  other arithmetic  0.97 us (1%)
    all_to_all x1, waiting for transfers between devices, on_device(): lax.all_to_all(outgoing.reshape(devices, CAP, 128), AXES, split_axis=0, c...  13.3 us
    pallas_call x1, Pallas kernels, on_device(): pl.pallas_call(land_kernel, grid=(1,), in_specs=[whole(slots, 128), whole...  11.8 us
    all_to_all x1, starting transfers between devices, on_device(): lax.all_to_all(wanted, AXES, split_axis=0, concat_axis=0, tiled=True)  11.5 us
    unnamed x32, local copies, waits for them, and re-layouts  9.18 us
    pallas_call x2, Pallas kernels, mix(): pl.pallas_call(functools.partial(mix_kernel, half, out_half), grid=(1,),...  8.29 us
    all_to_all x1, waiting for transfers between devices, on_device(): lax.all_to_all(reply.reshape(devices, CAP, 128), AXES, split_axis=0, conc...  6.49 us
    all_to_all x1, starting transfers between devices, on_device(): lax.all_to_all(reply.reshape(devices, CAP, 128), AXES, split_axis=0, conc...  5.11 us
    all_to_all x1, starting transfers between devices, on_device(): lax.all_to_all(outgoing.reshape(devices, CAP, 128), AXES, split_axis=0, c...  4.82 us
  transfers between devices with their start and end apart: 3, of which 3 were waited for; matrix products, arithmetic and copies ran while one was open for 1% of the time, Pallas kernels for 15%

profile of v1, /device:TPU:1, one launch (start us, length us, event | category | flops | bytes accessed | tf_op | source)
XLA Modules:
  0.0 90.0 jit_solution(11238234236405833614)
XLA Ops:
  0.6 1.9 %shard_map.157 = (s32[128,128]{1,0:T(8,128)}, s32[4,256]{1,0:T(4,128)}, s32[256,8]{1,0:T(8,128)}) custom-call(s32[4,256]{1,0:T(4,128)} %bitcast.21, s32[4,256]{1,0:T(4,128)} %bitcast.22), custom_call_target="tpu_custom_call" | custom-call | tf_op jit(solution)/shard_map/pallas_call | solution.py:493
  2.5 11.5 %all-to-all-start = ((s32[128,1,128]{2,1,0:T(1,128)}), s32[128,1,128]{2,1,0:T(1,128)S(1)}, u32[]{:S(2)}, u32[]{:S(2)}) async-start(s32[128,1,128]{2,1,0:T(1,128)} %bitcast.20), calls=%async_computation | async-start | bytes 131072 | tf_op jit(solution)/shard_map/all_to_all | solution.py:503
  14.1 0.8 copy-done.4
  14.9 0.7 copy-done.6
  15.5 3.2 %shard_map.158 = (f32[8,4096]{1,0:T(8,128)S(1)}, bf16[256,256]{1,0:T(8,128)(2,1)S(1)}) custom-call(f32[1,128]{1,0:T(1,128)S(1)} %bitcast.19, bf16[4096,512]{1,0:T(8,128)(2,1)} %state_ref.2, f32[4,4096]{1,0:T(4,128)S(1)} %copy-done.4), custom_call_target="tpu_custom_call" | custom-call | flops 134217728 | bytes 4194304 | tf_op jit(solution)/shard_map/pallas_call | solution.py:506
  18.7 4.7 %all-to-all-done = s32[128,1,128]{2,1,0:T(1,128)S(1)} async-done(((s32[128,1,128]{2,1,0:T(1,128)}), s32[128,1,128]{2,1,0:T(1,128)S(1)}, u32[]{:S(2)}, u32[]{:S(2)}) %all-to-all-start) | async-done | bytes 65568 | tf_op jit(solution)/shard_map/all_to_all | solution.py:503
  23.4 1.7 %shard_map.159 = f32[2048,128]{1,0:T(8,128)} custom-call(s32[128,128]{1,0:T(8,128)S(1)} %bitcast.16, bf16[256,256]{1,0:T(8,128)(2,1)S(1)} %get-tuple-element.44.blocks_ref), custom_call_target="tpu_custom_call" | custom-call | flops 268435456 | bytes 1048576 | tf_op jit(solution)/shard_map/pallas_call | solution.py:528
  25.1 5.1 %all-to-all-start.1 = ((f32[128,16,128]{2,1,0:T(8,128)}), f32[128,16,128]{2,1,0:T(8,128)S(1)}, u32[]{:S(2)}, u32[]{:S(2)}) async-start(f32[128,16,128]{2,1,0:T(8,128)} %bitcast.6), calls=%async_computation.1 | async-start | bytes 2097152 | tf_op jit(solution)/shard_map/all_to_all | solution.py:537
  30.2 2.2 %copy-done = bf16[4096,512]{1,0:T(8,128)(2,1)S(1)} copy-done((bf16[4096,512]{1,0:T(8,128)(2,1)S(1)}, bf16[4096,512]{1,0:T(8,128)(2,1)}, u32[]{:S(2)}) %copy-start) | copy-done | bytes 4194328
  32.4 4.5 %shard_map.160.kept_ref = bf16[4096,512]{1,0:T(8,128)(2,1)} custom-call(bf16[4,128,128]{2,1,0:T(8,128)(2,1)S(1)} %copy-done.3, bf16[4096,512]{1,0:T(8,128)(2,1)S(1)} %copy-done), custom_call_target="tpu_custom_call" | custom-call | flops 2147483648 | bytes 4194304 | tf_op jit(solution)/shard_map/pallas_call | solution.py:451
  37.0 1.0 %maximum_divide_fusion.incidence_ref = f32[256,128]{1,0:T(8,128)S(1)} fusion(s32[256,128]{1,0:T(8,128)S(1)} %copy-done.12, s32[256,128]{1,0:T(8,128)S(1)} %copy-done.13, f32[256]{0:T(256)S(1)} %copy-done.15, f32[256]{0:T(256)S(1)} %subtract_sqrt_fusion, f32[256]{0:T(256)S(1)} %copy-done.14), kind=kLoop, calls=%fused_computation | loop fusion | flops 360448 | bytes 396288 | tf_op jit(solution)/shard_map/div | solution.py:547
  38.0 0.0 copy-start.8
  38.0 0.0 copy-start.9
  38.0 1.6 %shard_map.161 = (bf16[16384,256]{1,0:T(8,128)(2,1)S(1)}, f32[256,128]{1,0:T(8,128)S(1)}) custom-call(f32[16384,128]{1,0:T(8,128)S(1)} %bitcast.13), custom_call_target="tpu_custom_call" | custom-call | flops 16777216 | bytes 16777216 | tf_op jit(solution)/shard_map/pallas_call | solution.py:556
  39.6 3.3 %copy-done.7 = bf16[16384,256]{1,0:T(8,128)(2,1)} copy-done((bf16[16384,256]{1,0:T(8,128)(2,1)}, bf16[16384,256]{1,0:T(8,128)(2,1)S(1)}, u32[]{:S(2)}) %copy-start.7) | copy-done | bytes 8388632
  42.9 6.5 %all-to-all-done.1 = f32[128,16,128]{2,1,0:T(8,128)S(1)} async-done(((f32[128,16,128]{2,1,0:T(8,128)}), f32[128,16,128]{2,1,0:T(8,128)S(1)}, u32[]{:S(2)}, u32[]{:S(2)}) %all-to-all-start.1) | async-done | bytes 1048608 | tf_op jit(solution)/shard_map/all_to_all | solution.py:537
  49.4 11.8 %shard_map.162 = (f32[256,128]{1,0:T(8,128)}, f32[2048,128]{1,0:T(8,128)}) custom-call(f32[2048,128]{1,0:T(8,128)S(1)} %bitcast.15, s32[4,256]{1,0:T(4,128)S(1)} %copy-done.11, s32[256,8]{1,0:T(8,128)S(1)} %copy-done.10, bf16[16384,256]{1,0:T(8,128)(2,1)} %copy-done.7, f32[256,128]{1,0:T(8,128)S(1)} %get-tuple-element.59.inverse_ref, ...), custom_call_target="tpu_custom_call" | custom-call | flops 4294967296 | bytes 8388608 | tf_op jit(solution)/shard_map/pallas_call | solution.py:575
  61.2 4.8 %all-to-all-start.2 = ((f32[128,16,128]{2,1,0:T(8,128)}), f32[128,16,128]{2,1,0:T(8,128)S(1)}, u32[]{:S(2)}, u32[]{:S(2)}) async-start(f32[128,16,128]{2,1,0:T(8,128)} %bitcast.9), calls=%async_computation.2 | async-start | bytes 2097152 | tf_op jit(solution)/shard_map/all_to_all | solution.py:603
  66.1 0.1 shard_map.164.ocean_ref
  66.1 0.0 copy-start.1
  66.1 2.2 %copy-done.1 = bf16[4096,512]{1,0:T(8,128)(2,1)S(1)} copy-done((bf16[4096,512]{1,0:T(8,128)(2,1)S(1)}, bf16[4096,512]{1,0:T(8,128)(2,1)}, u32[]{:S(2)}) %copy-start.1) | copy-done | bytes 4194328
  68.3 3.7 %shard_map.163.mixed_ref = bf16[4096,256]{1,0:T(8,128)(2,1)S(1)} custom-call(bf16[4,128,128]{2,1,0:T(8,128)(2,1)S(1)} %copy-done.3, bf16[4096,512]{1,0:T(8,128)(2,1)S(1)} %copy-done.1), custom_call_target="tpu_custom_call" | custom-call | flops 2147483648 | bytes 4194304 | tf_op jit(solution)/shard_map/pallas_call | solution.py:451
  72.1 13.3 %all-to-all-done.2 = f32[128,16,128]{2,1,0:T(8,128)S(1)} async-done(((f32[128,16,128]{2,1,0:T(8,128)}), f32[128,16,128]{2,1,0:T(8,128)S(1)}, u32[]{:S(2)}, u32[]{:S(2)}) %all-to-all-start.2) | async-done | bytes 1048608 | tf_op jit(solution)/shard_map/all_to_all | solution.py:603
  85.3 4.5 %shard_map.165 = (bf16[4096,512]{1,0:T(8,128)(2,1)}, f32[8,4096]{1,0:T(8,128)}) custom-call(f32[2048,128]{1,0:T(8,128)S(1)} %bitcast.14, s32[128,128]{1,0:T(8,128)S(1)} %bitcast.17, f32[8,4096]{1,0:T(8,128)S(1)} %shard_map.164.ocean_ref, bf16[4096,256]{1,0:T(8,128)(2,1)S(1)} %shard_map.163.mixed_ref, ...), custom_call_target="tpu_custom_call", output_to_operand_aliasing={{0}: (4, {})} | custom-call | tf_op jit(solution)/shard_map/pallas_call | solution.py:616
  (25 shorter events, 0.1 us)
Async XLA Ops:
  0.6 29.6 %copy-start.3 = (bf16[4,128,128]{2,1,0:T(8,128)(2,1)S(1)}, bf16[4,128,128]{2,1,0:T(8,128)(2,1)}, u32[]{:S(2)}) copy-start(bf16[4,128,128]{2,1,0:T(8,128)(2,1)} %mixing_ref.3) | copy-start | bytes 393220
  2.5 20.8 %all-to-all-start = ((s32[128,1,128]{2,1,0:T(1,128)}), s32[128,1,128]{2,1,0:T(1,128)S(1)}, u32[]{:S(2)}, u32[]{:S(2)}) async-start(s32[128,1,128]{2,1,0:T(1,128)} %bitcast.20), calls=%async_computation | async-start | bytes 131072 | tf_op jit(solution)/shard_map/all_to_all | solution.py:503
  14.0 0.8 copy-start.4
  14.9 0.7 copy-start.6
  25.1 11.9 %copy-start.14 = (f32[256]{0:T(256)S(1)}, f32[256]{0:T(256)}, u32[]{:S(2)}) copy-start(f32[256]{0:T(256)} %param.26) | copy-start | bytes 3076
  25.1 11.9 %copy-start.13 = (s32[256,128]{1,0:T(8,128)S(1)}, s32[256,128]{1,0:T(8,128)}, u32[]{:S(2)}) copy-start(s32[256,128]{1,0:T(8,128)} %param.22) | copy-start | bytes 393220
  25.1 24.3 %all-to-all-start.1 = ((f32[128,16,128]{2,1,0:T(8,128)}), f32[128,16,128]{2,1,0:T(8,128)S(1)}, u32[]{:S(2)}, u32[]{:S(2)}) async-start(f32[128,16,128]{2,1,0:T(8,128)} %bitcast.6), calls=%async_computation.1 | async-start | bytes 2097152 | tf_op jit(solution)/shard_map/all_to_all | solution.py:537
  30.2 2.2 %copy-start = (bf16[4096,512]{1,0:T(8,128)(2,1)S(1)}, bf16[4096,512]{1,0:T(8,128)(2,1)}, u32[]{:S(2)}) copy-start(bf16[4096,512]{1,0:T(8,128)(2,1)} %state_ref.2) | copy-start | bytes 12582916
  32.4 4.6 %copy-start.12 = (s32[256,128]{1,0:T(8,128)S(1)}, s32[256,128]{1,0:T(8,128)}, u32[]{:S(2)}) copy-start(s32[256,128]{1,0:T(8,128)} %param.23) | copy-start | bytes 393220
  32.4 4.6 %copy-start.15 = (f32[256]{0:T(256)S(1)}, f32[256]{0:T(256)}, u32[]{:S(2)}) copy-start(f32[256]{0:T(256)} %param.27) | copy-start | bytes 3076
  32.4 5.6 %copy-start.2 = (f32[256,64,128]{2,1,0:T(8,128)S(1)}, f32[256,64,128]{2,1,0:T(8,128)}, u32[]{:S(2)}) copy-start(f32[256,64,128]{2,1,0:T(8,128)} %param.21) | copy-start | bytes 25165828
  38.0 11.4 %copy-start.8 = (f32[256,128]{1,0:T(8,128)S(1)}, f32[256,128]{1,0:T(8,128)}, u32[]{:S(2)}) copy-start(f32[256,128]{1,0:T(8,128)} %sky_ref.1) | copy-start | bytes 393220
  38.0 11.4 %copy-start.9 = (f32[256,128]{1,0:T(8,128)S(1)}, f32[256,128]{1,0:T(8,128)}, u32[]{:S(2)}) copy-start(f32[256,128]{1,0:T(8,128)} %albedo_ref.1) | copy-start | bytes 393220
  38.0 11.4 %copy-start.10 = (s32[256,8]{1,0:T(8,128)S(1)}, s32[256,8]{1,0:T(8,128)}, u32[]{:S(2)}) copy-start(s32[256,8]{1,0:T(8,128)} %get-tuple-element.57.col_ref) | copy-start | bytes 24580
  38.0 11.4 %copy-start.11 = (s32[4,256]{1,0:T(4,128)S(1)}, s32[4,256]{1,0:T(4,128)}, u32[]{:S(2)}) copy-start(s32[4,256]{1,0:T(4,128)} %get-tuple-element.56.row_ref) | copy-start | bytes 12292
  39.6 3.3 %copy-start.7 = (bf16[16384,256]{1,0:T(8,128)(2,1)}, bf16[16384,256]{1,0:T(8,128)(2,1)S(1)}, u32[]{:S(2)}) copy-start(bf16[16384,256]{1,0:T(8,128)(2,1)S(1)} %get-tuple-element.58.both_ref) | copy-start | bytes 25165828
  49.4 16.7 %copy-start.5 = (s32[4096]{0:T(1024)S(1)}, s32[4096]{0:T(1024)}, u32[]{:S(2)}) copy-start(s32[4096]{0:T(1024)} %param.18) | copy-start | bytes 49156
  61.2 24.1 %all-to-all-start.2 = ((f32[128,16,128]{2,1,0:T(8,128)}), f32[128,16,128]{2,1,0:T(8,128)S(1)}, u32[]{:S(2)}, u32[]{:S(2)}) async-start(f32[128,16,128]{2,1,0:T(8,128)} %bitcast.9), calls=%async_computation.2 | async-start | bytes 2097152 | tf_op jit(solution)/shard_map/all_to_all | solution.py:603
  66.1 2.2 %copy-start.1 = (bf16[4096,512]{1,0:T(8,128)(2,1)S(1)}, bf16[4096,512]{1,0:T(8,128)(2,1)}, u32[]{:S(2)}) copy-start(bf16[4096,512]{1,0:T(8,128)(2,1)} %state_ref.2) | copy-start | bytes 12582916

commit v2 on v1

--- a/solution.py
+++ b/solution.py
@@ -37,6 +37,10 @@
 
 def matmul_nt(left, right):
     return lax.dot_general(left, right, (((1,), (1,)), ((), ())), preferred_element_type=F32)
+
+
+def part_of(index, size):
+    return pl.ds(index * size, size)
 
 
 def flag(condition):
@@ -302,9 +306,9 @@
     left = iota((8, 128), 1) < KDIM
     zero = jnp.zeros((8, 128), F32)
 
-    def take(group, carry):
-        weights = held_ref[pl.ds(pl.multiple_of(group * 256, 256), 256), :]
-        need = need_ref[pl.ds(pl.multiple_of(group * 16, 16), 16), :]
+    def take(group):
+        weights = held_ref[part_of(group, 256), :]
+        need = need_ref[part_of(group, 16), :]
         rows = []
         for part in high_low(need):
             for half in range(2):
@@ -314,13 +318,13 @@
                         jnp.concatenate([masked, zero] if half == 0 else [zero, masked], axis=1)
                     )
         product = fold(matmul(jnp.concatenate(rows, axis=0).astype(BF16), weights))
-        raw_ref[pl.ds(pl.multiple_of(group * 32, 32), 32), :] = product[0:32] + product[32:64]
-        return carry
+        raw_ref[part_of(group, 32), :] = product[0:32] + product[32:64]
 
     size = tiles // 4 // parts
     for part in range(parts):
         copies[part].wait()
-        lax.fori_loop(part * size, (part + 1) * size, take, 0, unroll=8)
+        for group in range(part * size, (part + 1) * size):
+            take(group)
 
     inverse = inverse_ref[...]
     fields = [raw_ref[pl.ds(index, tiles, stride=NF), :] * inverse for index in range(NF)]
@@ -348,29 +352,29 @@
     for index in range(NF):
         raw_ref[pl.ds(index, tiles, stride=NF), :] = fluxes[index] * inverse
 
-    def give(group, carry):
-        flux = raw_ref[pl.ds(pl.multiple_of(group * 32, 32), 32), :]
+    def give(group):
+        flux = raw_ref[part_of(group, 32), :]
         high, low = high_low(flux)
         stacked = jnp.concatenate([high, low], axis=0).astype(BF16)
         stacked = jnp.concatenate([stacked, stacked], axis=1)
-        weights = held_ref[pl.ds(pl.multiple_of(group * 256, 256), 256), :]
+        weights = held_ref[part_of(group, 256), :]
         product = matmul_nt(stacked, weights)
         product = product[0:32] + product[32:64]
-        need_ref[pl.ds(pl.multiple_of(group * 16, 16), 16), :] = jnp.concatenate(
+        need_ref[part_of(group, 16), :] = jnp.concatenate(
             [
                 jnp.where(left, product[0:8, 0:128], product[8:16, 0:128]),
                 jnp.where(left, product[16:24, 128:256], product[24:32, 128:256]),
             ],
             axis=0,
         )
-        return carry
-
-    lax.fori_loop(0, tiles // 4, give, 0, unroll=16)
+
+    for group in range(tiles // 4):
+        give(group)
     need_ref[...] = block_swap(need_ref[...])
     given = jnp.concatenate(
         [pair(need_ref[pl.ds(ref, tiles, stride=REF), :]) for ref in range(REF)], axis=0
     )
-    size = 256
+    size = 512
 
     def place(index, carry):
         start = pl.multiple_of(index * size, size)
@@ -406,19 +410,23 @@
     swapped = block_swap(fold(part))
     parts = sems.shape[0]
     size = held_ref.shape[0] // parts
-    lane = iota((128, 128), 1)
-    copies = []
+    row, lane = iota((16, 256), 0) & 7, iota((16, 256), 1)
+    first, second = (row == 0) & (lane == 0), (row == 6) & (lane == 128)
+    picks = flag(first | second)
+    tens, copies = [], []
     for index in range(parts):
         for start in range(index * size, index * size + size, 128):
             columns = slice(start, start + 128)
             flux = swapped[start // 16 : start // 16 + 8] + ocean_ref[:, columns]
             flux_ref[:, columns] = flux
-            turned = jnp.transpose(flux)
-            for half, row in ((0, 0), (1, 6)):
-                lanes = slice(half * 128, half * 128 + 128)
-                added = jnp.where(lane == 0, 0.1 * turned[:, row : row + 1], 0.0)
-                state = mixed_ref[columns, lanes].astype(F32)
-                held_ref[columns, lanes] = (state + added).astype(BF16)
+            tens.append(0.1 * flux)
+        high, low = high_low(jnp.concatenate(tens[-size // 128 :], axis=1))
+        table = jnp.concatenate([high, low], axis=0).astype(BF16)
+        added = lax.dot_general(
+            table, picks, (((0,), (0,)), ((), ())), preferred_element_type=F32
+        )
+        rows = slice(index * size, index * size + size)
+        held_ref[rows, :] = (mixed_ref[rows, :].astype(F32) + added).astype(BF16)
         span = pl.ds(index * size, size)
         copy = pltpu.make_async_copy(
             held_ref.at[span, :], out_ref.at[span, pl.ds(0, 256)], sems.at[index]
@@ -594,7 +602,7 @@
             pltpu.VMEM((requests, 128), F32),
             pltpu.VMEM((tiles * NF, 128), F32),
             pltpu.VMEM((tiles * KDIM, 256), BF16),
-            pltpu.SemaphoreType.DMA((8,)),
+            pltpu.SemaphoreType.DMA((4,)),
         ],
         compiler_params=params(50, 1),
         cost_estimate=cost(4 * requests * slots * 256 * 2, tiles * KDIM * UNIT * 4),
@@ -630,7 +638,7 @@
         ),
         scratch_shapes=[
             pltpu.VMEM((columns, 256), BF16),
-            pltpu.SemaphoreType.DMA((parts,)),
+            pltpu.SemaphoreType.DMA((8,)),
         ],
         input_output_aliases={4: 0},
         compiler_params=params(16, 1),

time: 90.4 us -> 87.3 us (0.966)
  Pallas kernels: 32.9 us -> 29.8 us
    pallas_call x1, Pallas kernels: 11.8 us -> 9.14 us  [on_device(): pl.pallas_call(land_kernel, grid=(1,), in_specs=[whole(slots, 128), whole...]
where the time goes in v2:
time: 87.3 us; the launch traced here: 86.9 us
  Pallas kernels  29.8 us (34%)
  waiting for transfers between devices  24.4 us (28%)
  starting transfers between devices  21.4 us (25%)
  local copies, waits for them, and re-layouts  9.18 us (11%)
  between operations  1.03 us (1%)
  other arithmetic  0.97 us (1%)
    all_to_all x1, waiting for transfers between devices, on_device(): lax.all_to_all(outgoing.reshape(devices, CAP, 128), AXES, split_axis=0, c...  13.3 us
    all_to_all x1, starting transfers between devices, on_device(): lax.all_to_all(wanted, AXES, split_axis=0, concat_axis=0, tiled=True)  11.5 us
    unnamed x32, local copies, waits for them, and re-layouts  9.18 us
    pallas_call x1, Pallas kernels, on_device(): pl.pallas_call(land_kernel, grid=(1,), in_specs=[whole(slots, 128), whole...  9.14 us
    pallas_call x2, Pallas kernels, mix(): pl.pallas_call(functools.partial(mix_kernel, half, out_half), grid=(1,),...  8.29 us
    all_to_all x1, waiting for transfers between devices, on_device(): lax.all_to_all(reply.reshape(devices, CAP, 128), AXES, split_axis=0, conc...  6.49 us
    all_to_all x1, starting transfers between devices, on_device(): lax.all_to_all(reply.reshape(devices, CAP, 128), AXES, split_axis=0, conc...  5.11 us
    all_to_all x1, starting transfers between devices, on_device(): lax.all_to_all(outgoing.reshape(devices, CAP, 128), AXES, split_axis=0, c...  4.8 us
  transfers between devices with their start and end apart: 3, of which 3 were waited for; matrix products, arithmetic and copies ran while one was open for 1% of the time, Pallas kernels for 15%

profile of v2, /device:TPU:1, one launch (start us, length us, event | category | flops | bytes accessed | tf_op | source)
XLA Modules:
  0.0 86.9 jit_solution(14527853246443703805)
XLA Ops:
  0.6 1.9 %shard_map.157 = (s32[128,128]{1,0:T(8,128)}, s32[4,256]{1,0:T(4,128)}, s32[256,8]{1,0:T(8,128)}) custom-call(s32[4,256]{1,0:T(4,128)} %bitcast.21, s32[4,256]{1,0:T(4,128)} %bitcast.22), custom_call_target="tpu_custom_call" | custom-call | tf_op jit(solution)/shard_map/pallas_call | solution.py:501
  2.5 11.5 %all-to-all-start = ((s32[128,1,128]{2,1,0:T(1,128)}), s32[128,1,128]{2,1,0:T(1,128)S(1)}, u32[]{:S(2)}, u32[]{:S(2)}) async-start(s32[128,1,128]{2,1,0:T(1,128)} %bitcast.20), calls=%async_computation | async-start | bytes 131072 | tf_op jit(solution)/shard_map/all_to_all | solution.py:511
  14.0 0.0 copy-start.4
  14.1 0.8 copy-done.4
  14.9 0.7 copy-done.6
  15.5 3.2 %shard_map.158 = (f32[8,4096]{1,0:T(8,128)S(1)}, bf16[256,256]{1,0:T(8,128)(2,1)S(1)}) custom-call(f32[1,128]{1,0:T(1,128)S(1)} %bitcast.19, bf16[4096,512]{1,0:T(8,128)(2,1)} %state_ref.2, f32[4,4096]{1,0:T(4,128)S(1)} %copy-done.4), custom_call_target="tpu_custom_call" | custom-call | flops 134217728 | bytes 4194304 | tf_op jit(solution)/shard_map/pallas_call | solution.py:514
  18.7 4.7 %all-to-all-done = s32[128,1,128]{2,1,0:T(1,128)S(1)} async-done(((s32[128,1,128]{2,1,0:T(1,128)}), s32[128,1,128]{2,1,0:T(1,128)S(1)}, u32[]{:S(2)}, u32[]{:S(2)}) %all-to-all-start) | async-done | bytes 65568 | tf_op jit(solution)/shard_map/all_to_all | solution.py:511
  23.4 1.7 %shard_map.159 = f32[2048,128]{1,0:T(8,128)} custom-call(s32[128,128]{1,0:T(8,128)S(1)} %bitcast.16, bf16[256,256]{1,0:T(8,128)(2,1)S(1)} %get-tuple-element.44.blocks_ref), custom_call_target="tpu_custom_call" | custom-call | flops 268435456 | bytes 1048576 | tf_op jit(solution)/shard_map/pallas_call | solution.py:536
  25.1 5.1 %all-to-all-start.1 = ((f32[128,16,128]{2,1,0:T(8,128)}), f32[128,16,128]{2,1,0:T(8,128)S(1)}, u32[]{:S(2)}, u32[]{:S(2)}) async-start(f32[128,16,128]{2,1,0:T(8,128)} %bitcast.6), calls=%async_computation.1 | async-start | bytes 2097152 | tf_op jit(solution)/shard_map/all_to_all | solution.py:545
  30.2 2.2 %copy-done = bf16[4096,512]{1,0:T(8,128)(2,1)S(1)} copy-done((bf16[4096,512]{1,0:T(8,128)(2,1)S(1)}, bf16[4096,512]{1,0:T(8,128)(2,1)}, u32[]{:S(2)}) %copy-start) | copy-done | bytes 4194328
  32.4 4.5 %shard_map.160.kept_ref = bf16[4096,512]{1,0:T(8,128)(2,1)} custom-call(bf16[4,128,128]{2,1,0:T(8,128)(2,1)S(1)} %copy-done.3, bf16[4096,512]{1,0:T(8,128)(2,1)S(1)} %copy-done), custom_call_target="tpu_custom_call" | custom-call | flops 2147483648 | bytes 4194304 | tf_op jit(solution)/shard_map/pallas_call | solution.py:459
  37.0 1.0 %maximum_divide_fusion.incidence_ref = f32[256,128]{1,0:T(8,128)S(1)} fusion(s32[256,128]{1,0:T(8,128)S(1)} %copy-done.12, s32[256,128]{1,0:T(8,128)S(1)} %copy-done.13, f32[256]{0:T(256)S(1)} %copy-done.15, f32[256]{0:T(256)S(1)} %subtract_sqrt_fusion, f32[256]{0:T(256)S(1)} %copy-done.14), kind=kLoop, calls=%fused_computation | loop fusion | flops 360448 | bytes 396288 | tf_op jit(solution)/shard_map/div | solution.py:555
  38.0 0.0 copy-start.9
  38.0 0.0 copy-start.10
  38.0 1.6 %shard_map.161 = (bf16[16384,256]{1,0:T(8,128)(2,1)S(1)}, f32[256,128]{1,0:T(8,128)S(1)}) custom-call(f32[16384,128]{1,0:T(8,128)S(1)} %bitcast.13), custom_call_target="tpu_custom_call" | custom-call | flops 16777216 | bytes 16777216 | tf_op jit(solution)/shard_map/pallas_call | solution.py:564
  39.6 3.3 %copy-done.7 = bf16[16384,256]{1,0:T(8,128)(2,1)} copy-done((bf16[16384,256]{1,0:T(8,128)(2,1)}, bf16[16384,256]{1,0:T(8,128)(2,1)S(1)}, u32[]{:S(2)}) %copy-start.7) | copy-done | bytes 8388632
  42.9 6.5 %all-to-all-done.1 = f32[128,16,128]{2,1,0:T(8,128)S(1)} async-done(((f32[128,16,128]{2,1,0:T(8,128)}), f32[128,16,128]{2,1,0:T(8,128)S(1)}, u32[]{:S(2)}, u32[]{:S(2)}) %all-to-all-start.1) | async-done | bytes 1048608 | tf_op jit(solution)/shard_map/all_to_all | solution.py:545
  49.4 9.1 %shard_map.162 = (f32[256,128]{1,0:T(8,128)}, f32[2048,128]{1,0:T(8,128)}) custom-call(f32[2048,128]{1,0:T(8,128)S(1)} %bitcast.15, s32[4,256]{1,0:T(4,128)S(1)} %copy-done.11, s32[256,8]{1,0:T(8,128)S(1)} %copy-done.10, bf16[16384,256]{1,0:T(8,128)(2,1)} %copy-done.7, f32[256,128]{1,0:T(8,128)S(1)} %get-tuple-element.59.inverse_ref, ...), custom_call_target="tpu_custom_call" | custom-call | flops 4294967296 | bytes 8388608 | tf_op jit(solution)/shard_map/pallas_call | solution.py:583
  58.5 4.8 %all-to-all-start.2 = ((f32[128,16,128]{2,1,0:T(8,128)}), f32[128,16,128]{2,1,0:T(8,128)S(1)}, u32[]{:S(2)}, u32[]{:S(2)}) async-start(f32[128,16,128]{2,1,0:T(8,128)} %bitcast.9), calls=%async_computation.2 | async-start | bytes 2097152 | tf_op jit(solution)/shard_map/all_to_all | solution.py:611
  63.4 0.1 shard_map.164.ocean_ref
  63.4 2.2 %copy-done.1 = bf16[4096,512]{1,0:T(8,128)(2,1)S(1)} copy-done((bf16[4096,512]{1,0:T(8,128)(2,1)S(1)}, bf16[4096,512]{1,0:T(8,128)(2,1)}, u32[]{:S(2)}) %copy-start.1) | copy-done | bytes 4194328
  65.6 3.7 %shard_map.163.mixed_ref = bf16[4096,256]{1,0:T(8,128)(2,1)S(1)} custom-call(bf16[4,128,128]{2,1,0:T(8,128)(2,1)S(1)} %copy-done.3, bf16[4096,512]{1,0:T(8,128)(2,1)S(1)} %copy-done.1), custom_call_target="tpu_custom_call" | custom-call | flops 2147483648 | bytes 4194304 | tf_op jit(solution)/shard_map/pallas_call | solution.py:459
  69.4 13.3 %all-to-all-done.2 = f32[128,16,128]{2,1,0:T(8,128)S(1)} async-done(((f32[128,16,128]{2,1,0:T(8,128)}), f32[128,16,128]{2,1,0:T(8,128)S(1)}, u32[]{:S(2)}, u32[]{:S(2)}) %all-to-all-start.2) | async-done | bytes 1048608 | tf_op jit(solution)/shard_map/all_to_all | solution.py:611
  82.7 4.1 %shard_map.165 = (bf16[4096,512]{1,0:T(8,128)(2,1)}, f32[8,4096]{1,0:T(8,128)}) custom-call(f32[2048,128]{1,0:T(8,128)S(1)} %bitcast.14, s32[128,128]{1,0:T(8,128)S(1)} %bitcast.17, f32[8,4096]{1,0:T(8,128)S(1)} %shard_map.164.ocean_ref, bf16[4096,256]{1,0:T(8,128)(2,1)S(1)} %shard_map.163.mixed_ref, ...), custom_call_target="tpu_custom_call", output_to_operand_aliasing={{0}: (4, {})} | custom-call | tf_op jit(solution)/shard_map/pallas_call | solution.py:624
  (25 shorter events, 0.1 us)
Async XLA Ops:
  0.6 29.6 %copy-start.3 = (bf16[4,128,128]{2,1,0:T(8,128)(2,1)S(1)}, bf16[4,128,128]{2,1,0:T(8,128)(2,1)}, u32[]{:S(2)}) copy-start(bf16[4,128,128]{2,1,0:T(8,128)(2,1)} %mixing_ref.3) | copy-start | bytes 393220
  2.5 20.8 %all-to-all-start = ((s32[128,1,128]{2,1,0:T(1,128)}), s32[128,1,128]{2,1,0:T(1,128)S(1)}, u32[]{:S(2)}, u32[]{:S(2)}) async-start(s32[128,1,128]{2,1,0:T(1,128)} %bitcast.20), calls=%async_computation | async-start | bytes 131072 | tf_op jit(solution)/shard_map/all_to_all | solution.py:511
  14.0 0.8 copy-start.4
  14.9 0.7 copy-start.6
  25.1 11.9 %copy-start.14 = (f32[256]{0:T(256)S(1)}, f32[256]{0:T(256)}, u32[]{:S(2)}) copy-start(f32[256]{0:T(256)} %param.26) | copy-start | bytes 3076
  25.1 11.9 %copy-start.13 = (s32[256,128]{1,0:T(8,128)S(1)}, s32[256,128]{1,0:T(8,128)}, u32[]{:S(2)}) copy-start(s32[256,128]{1,0:T(8,128)} %param.22) | copy-start | bytes 393220
  25.1 24.3 %all-to-all-start.1 = ((f32[128,16,128]{2,1,0:T(8,128)}), f32[128,16,128]{2,1,0:T(8,128)S(1)}, u32[]{:S(2)}, u32[]{:S(2)}) async-start(f32[128,16,128]{2,1,0:T(8,128)} %bitcast.6), calls=%async_computation.1 | async-start | bytes 2097152 | tf_op jit(solution)/shard_map/all_to_all | solution.py:545
  30.2 2.2 %copy-start = (bf16[4096,512]{1,0:T(8,128)(2,1)S(1)}, bf16[4096,512]{1,0:T(8,128)(2,1)}, u32[]{:S(2)}) copy-start(bf16[4096,512]{1,0:T(8,128)(2,1)} %state_ref.2) | copy-start | bytes 12582916
  32.4 4.6 %copy-start.12 = (s32[256,128]{1,0:T(8,128)S(1)}, s32[256,128]{1,0:T(8,128)}, u32[]{:S(2)}) copy-start(s32[256,128]{1,0:T(8,128)} %param.23) | copy-start | bytes 393220
  32.4 4.6 %copy-start.15 = (f32[256]{0:T(256)S(1)}, f32[256]{0:T(256)}, u32[]{:S(2)}) copy-start(f32[256]{0:T(256)} %param.27) | copy-start | bytes 3076
  32.4 5.6 %copy-start.2 = (f32[256,64,128]{2,1,0:T(8,128)S(1)}, f32[256,64,128]{2,1,0:T(8,128)}, u32[]{:S(2)}) copy-start(f32[256,64,128]{2,1,0:T(8,128)} %param.21) | copy-start | bytes 25165828
  38.0 11.4 %copy-start.8 = (f32[256,128]{1,0:T(8,128)S(1)}, f32[256,128]{1,0:T(8,128)}, u32[]{:S(2)}) copy-start(f32[256,128]{1,0:T(8,128)} %sky_ref.1) | copy-start | bytes 393220
  38.0 11.4 %copy-start.9 = (f32[256,128]{1,0:T(8,128)S(1)}, f32[256,128]{1,0:T(8,128)}, u32[]{:S(2)}) copy-start(f32[256,128]{1,0:T(8,128)} %albedo_ref.1) | copy-start | bytes 393220
  38.0 11.4 %copy-start.10 = (s32[256,8]{1,0:T(8,128)S(1)}, s32[256,8]{1,0:T(8,128)}, u32[]{:S(2)}) copy-start(s32[256,8]{1,0:T(8,128)} %get-tuple-element.57.col_ref) | copy-start | bytes 24580
  38.0 11.4 %copy-start.11 = (s32[4,256]{1,0:T(4,128)S(1)}, s32[4,256]{1,0:T(4,128)}, u32[]{:S(2)}) copy-start(s32[4,256]{1,0:T(4,128)} %get-tuple-element.56.row_ref) | copy-start | bytes 12292
  39.6 3.3 %copy-start.7 = (bf16[16384,256]{1,0:T(8,128)(2,1)}, bf16[16384,256]{1,0:T(8,128)(2,1)S(1)}, u32[]{:S(2)}) copy-start(bf16[16384,256]{1,0:T(8,128)(2,1)S(1)} %get-tuple-element.58.both_ref) | copy-start | bytes 25165828
  49.4 14.0 %copy-start.5 = (s32[4096]{0:T(1024)S(1)}, s32[4096]{0:T(1024)}, u32[]{:S(2)}) copy-start(s32[4096]{0:T(1024)} %param.18) | copy-start | bytes 49156
  58.5 24.1 %all-to-all-start.2 = ((f32[128,16,128]{2,1,0:T(8,128)}), f32[128,16,128]{2,1,0:T(8,128)S(1)}, u32[]{:S(2)}, u32[]{:S(2)}) async-start(f32[128,16,128]{2,1,0:T(8,128)} %bitcast.9), calls=%async_computation.2 | async-start | bytes 2097152 | tf_op jit(solution)/shard_map/all_to_all | solution.py:611
  63.4 2.2 %copy-start.1 = (bf16[4096,512]{1,0:T(8,128)(2,1)S(1)}, bf16[4096,512]{1,0:T(8,128)(2,1)}, u32[]{:S(2)}) copy-start(bf16[4096,512]{1,0:T(8,128)(2,1)} %state_ref.2) | copy-start | bytes 12582916

commit v3 on v2

--- a/solution.py
+++ b/solution.py
@@ -76,6 +76,18 @@
             moved = jnp.where(chunk_bit == 1, up, down)
         cube = jnp.where(row_bit == chunk_bit, cube, moved)
     return cube.reshape(values.shape)
+
+
+def shear(values):
+    return pltpu.roll(values, 0, 1, stride=16, stride_axis=0)
+
+
+def turned_swap(values):
+    cube = shear(values).reshape(values.shape[0] // 8, 8, 128)
+    chunk = iota(cube.shape, 2) >> 4
+    for reach in (1, 2, 4):
+        cube = jnp.where((chunk & reach) != 0, pltpu.roll(cube, 8 - reach, 1), cube)
+    return shear(cube.reshape(values.shape))
 
 
 def drivers(fields):
@@ -147,9 +159,14 @@
         wanted = wanted + matmul_nt(onehot, table)
         places.append(source * CAP + rank)
     want_ref[...] = wanted.astype(I32) - 1
-    for ref in range(REF):
-        row_ref[ref : ref + 1, :] = places[ref]
     stacked = jnp.concatenate(places + places, axis=0).astype(F32)
+    odd = (iota((1, tiles), 1) & 1) == 1
+    turned = [
+        jnp.where(odd, pltpu.roll(place, 1, 1), pltpu.roll(place, tiles - 1, 1))
+        for place in places[:0:-1]
+    ]
+    for ref, place in enumerate([places[0]] + turned):
+        row_ref[ref : ref + 1, :] = place
     col_ref[...] = jnp.transpose(stacked).astype(I32)
 
 
@@ -186,14 +203,32 @@
     blocks_ref[...] = pair(block_swap(jnp.concatenate(pieces, axis=0)))
 
 
-def reply_kernel(incoming_ref, blocks_ref, reply_ref):
-    devices, elements = incoming_ref.shape[0], blocks_ref.shape[0]
+def send_part(held, target, sems, part, size):
+    span = pl.ds(part * size, size)
+    copy = pltpu.make_async_copy(held.at[span, :], target.at[span, :], sems.at[part])
+    copy.start()
+    return copy
+
+
+def reply_kernel(incoming_ref, blocks_ref, reply_ref, held_ref, sems):
+    parts = sems.shape[0]
+    devices, elements = incoming_ref.shape[0] // parts, blocks_ref.shape[0]
     element = iota((devices, elements), 1)
     blocks = blocks_ref[...]
-    incoming = incoming_ref[...]
-    for slot in range(CAP):
-        select = flag(element == incoming[:, slot : slot + 1])
-        reply_ref[pl.ds(slot, devices, stride=CAP), :] = fold(matmul(select, blocks))
+    copies = []
+    for part in range(parts):
+        incoming = incoming_ref[part * devices : (part + 1) * devices, :]
+        select = jnp.concatenate(
+            [flag(element == incoming[:, slot : slot + 1]) for slot in range(CAP)], axis=0
+        )
+        values = fold(matmul(select, blocks))
+        for slot in range(CAP):
+            held_ref[pl.ds(part * devices * CAP + slot, devices, stride=CAP), :] = values[
+                slot * devices : (slot + 1) * devices
+            ]
+        copies.append(send_part(held_ref, reply_ref, sems, part, devices * CAP))
+    for copy in copies:
+        copy.wait()
 
 
 def prepare_kernel(w_ref, both_ref, inverse_ref):
@@ -301,7 +336,7 @@
     for ref in range(REF):
         pick = flag(slot == col_ref[:, ref : ref + 1])
         need_ref[pl.ds(ref, tiles, stride=REF), :] = fold(matmul(pick, arrived))
-    need_ref[...] = block_swap(need_ref[...])
+    need_ref[...] = turned_swap(need_ref[...])
 
     left = iota((8, 128), 1) < KDIM
     zero = jnp.zeros((8, 128), F32)
@@ -327,7 +362,9 @@
             take(group)
 
     inverse = inverse_ref[...]
-    fields = [raw_ref[pl.ds(index, tiles, stride=NF), :] * inverse for index in range(NF)]
+    fields = [
+        raw_ref[pl.ds((NF - index) % NF, tiles, stride=NF), :] * inverse for index in range(NF)
+    ]
     driven = drivers(fields)
     air_temp, air_humid, wind_speed, direct_sw, diffuse_sw, longwave, wetness = driven
     sky, albedo = sky_ref[...], albedo_ref[...]
@@ -350,7 +387,7 @@
     temp_ref[...] = surface
     fluxes = flux_list(surface, fields, driven, absorbed, albedo * shortwave, wetness)
     for index in range(NF):
-        raw_ref[pl.ds(index, tiles, stride=NF), :] = fluxes[index] * inverse
+        raw_ref[pl.ds((NF - index) % NF, tiles, stride=NF), :] = fluxes[index] * inverse
 
     def give(group):
         flux = raw_ref[part_of(group, 32), :]
@@ -370,7 +407,7 @@
 
     for group in range(tiles // 4):
         give(group)
-    need_ref[...] = block_swap(need_ref[...])
+    need_ref[...] = turned_swap(need_ref[...])
     given = jnp.concatenate(
         [pair(need_ref[pl.ds(ref, tiles, stride=REF), :]) for ref in range(REF)], axis=0
     )
@@ -407,7 +444,7 @@
             axis=0,
         )
         part = part + matmul(select, values)
-    swapped = block_swap(fold(part))
+    swapped = turned_swap(fold(part))
     parts = sems.shape[0]
     size = held_ref.shape[0] // parts
     row, lane = iota((16, 256), 0) & 7, iota((16, 256), 1)
@@ -535,18 +572,21 @@
 
     reply = pl.pallas_call(
         reply_kernel,
+        grid=(1,),
+        in_specs=[whole(devices, 128), whole(elements, 256)],
+        out_specs=pl.BlockSpec(memory_space=pltpu.HBM),
         out_shape=jax.ShapeDtypeStruct((slots, 128), F32),
-        compiler_params=params(16),
+        scratch_shapes=[pltpu.VMEM((slots, 128), F32), pltpu.SemaphoreType.DMA((4,))],
+        compiler_params=params(16, 1),
         cost_estimate=cost(slots * 256 * 256 * 2, slots * 512),
     )(incoming, blocks)
-    reply, atm_state, remap_w, slope_class, sun_cos = lax.optimization_barrier(
-        (reply, atm_state, remap_w, slope_class, sun_cos)
+    reply, remap_w, slope_class, sun_cos = lax.optimization_barrier(
+        (reply, remap_w, slope_class, sun_cos)
     )
     arrived = lax.all_to_all(
         reply.reshape(devices, CAP, 128), AXES, split_axis=0, concat_axis=0, tiled=True
     ).reshape(slots, 128)
 
-    kept = mix(mixing, atm_state, 1, 1)
     cosine = sun_cos[:, None]
     sine = jnp.sqrt(1.0 - cosine * cosine)
     slope_angle = slope_class.astype(F32) * 0.1
@@ -559,7 +599,6 @@
         )
         / cosine
     )
-    remap_w, kept, incidence = lax.optimization_barrier((remap_w, kept, incidence))
     rows = 4096
     both, inverse = pl.pallas_call(
         prepare_kernel,
@@ -576,8 +615,8 @@
         compiler_params=params(20, 1),
         cost_estimate=cost(tiles * KDIM * UNIT * 8, tiles * KDIM * UNIT * 8),
     )(remap_w.reshape(tiles * KDIM, UNIT))
-    arrived, kept, both, inverse, incidence = lax.optimization_barrier(
-        (arrived, kept, both, inverse, incidence)
+    arrived, both, inverse, incidence = lax.optimization_barrier(
+        (arrived, both, inverse, incidence)
     )
 
     land_temp, outgoing = pl.pallas_call(
@@ -613,13 +652,14 @@
     ).reshape(slots, 128)
 
     mixed = mix(mixing, atm_state, 0, None)
+    kept = mix(mixing, atm_state, 1, 1)
     ocean = pl.pallas_call(
         ocean_kernel,
         out_shape=jax.ShapeDtypeStruct((NF, columns), F32),
         compiler_params=params(16),
         cost_estimate=cost(columns * 100, columns * 64, columns * 4),
     )(forcing, ocean_mask.reshape(1, columns))
-    returned, mixed, ocean = lax.optimization_barrier((returned, mixed, ocean))
+    returned, mixed, kept, ocean = lax.optimization_barrier((returned, mixed, kept, ocean))
 
     atm_out, col_flux = pl.pallas_call(
         finish_kernel,

time: 87.3 us -> 86.7 us (level)
  local copies, waits for them, and re-layouts: 9.18 us -> 10.4 us
  waiting for transfers between devices: 24.4 us -> 23.3 us
    all_to_all x1, waiting for transfers between devices: 13.3 us -> 8.72 us  [on_device(): lax.all_to_all(outgoing.reshape(devices, CAP, 128), AXES, split_axis=0, c...]
    all_to_all x1, waiting for transfers between devices: 6.49 us -> 9.88 us  [on_device(): lax.all_to_all(reply.reshape(devices, CAP, 128), AXES, split_axis=0, conc...]
    unnamed x32 -> x30, local copies, waits for them, and re-layouts: 9.18 us -> 10.4 us
where the time goes in v3:
time: 86.7 us; the launch traced here: 86.3 us
  Pallas kernels  29.4 us (34%)
  waiting for transfers between devices  23.3 us (27%)
  starting transfers between devices  21.3 us (25%)
  local copies, waits for them, and re-layouts  10.4 us (12%)
  between operations  1.02 us (1%)
  other arithmetic  0.97 us (1%)
    all_to_all x1, starting transfers between devices, on_device(): lax.all_to_all(wanted, AXES, split_axis=0, concat_axis=0, tiled=True)  11.5 us
    unnamed x30, local copies, waits for them, and re-layouts  10.4 us
    all_to_all x1, waiting for transfers between devices, on_device(): lax.all_to_all(reply.reshape(devices, CAP, 128), AXES, split_axis=0, conc...  9.88 us
    pallas_call x1, Pallas kernels, on_device(): pl.pallas_call(land_kernel, grid=(1,), in_specs=[whole(slots, 128), whole...  9.18 us
    all_to_all x1, waiting for transfers between devices, on_device(): lax.all_to_all(outgoing.reshape(devices, CAP, 128), AXES, split_axis=0, c...  8.72 us
    pallas_call x2, Pallas kernels, mix(): pl.pallas_call(functools.partial(mix_kernel, half, out_half), grid=(1,),...  8.29 us
    all_to_all x1, starting transfers between devices, on_device(): lax.all_to_all(reply.reshape(devices, CAP, 128), AXES, split_axis=0, conc...  5.12 us
    all_to_all x1, waiting for transfers between devices, on_device(): lax.all_to_all(wanted, AXES, split_axis=0, concat_axis=0, tiled=True)  4.66 us
  transfers between devices with their start and end apart: 3, of which 3 were waited for; matrix products, arithmetic and copies ran while one was open for 1% of the time, Pallas kernels for 15%

profile of v3, /device:TPU:1, one launch (start us, length us, event | category | flops | bytes accessed | tf_op | source)
XLA Modules:
  0.0 86.3 jit_solution(14397460104566214585)
XLA Ops:
  0.6 1.9 %shard_map.157 = (s32[128,128]{1,0:T(8,128)}, s32[4,256]{1,0:T(4,128)}, s32[256,8]{1,0:T(8,128)}) custom-call(s32[4,256]{1,0:T(4,128)} %bitcast.21, s32[4,256]{1,0:T(4,128)} %bitcast.22), custom_call_target="tpu_custom_call" | custom-call | tf_op jit(solution)/shard_map/pallas_call | solution.py:538
  2.5 11.5 %all-to-all-start = ((s32[128,1,128]{2,1,0:T(1,128)}), s32[128,1,128]{2,1,0:T(1,128)S(1)}, u32[]{:S(2)}, u32[]{:S(2)}) async-start(s32[128,1,128]{2,1,0:T(1,128)} %bitcast.20), calls=%async_computation | async-start | bytes 131072 | tf_op jit(solution)/shard_map/all_to_all | solution.py:548
  14.0 0.0 copy-start.3
  14.0 0.8 copy-done.3
  14.8 0.7 copy-done.5
  15.5 3.2 %shard_map.158 = (f32[8,4096]{1,0:T(8,128)S(1)}, bf16[256,256]{1,0:T(8,128)(2,1)S(1)}) custom-call(f32[1,128]{1,0:T(1,128)S(1)} %bitcast.19, bf16[4096,512]{1,0:T(8,128)(2,1)} %state_ref.2, f32[4,4096]{1,0:T(4,128)S(1)} %copy-done.3), custom_call_target="tpu_custom_call" | custom-call | flops 134217728 | bytes 4194304 | tf_op jit(solution)/shard_map/pallas_call | solution.py:551
  18.7 4.7 %all-to-all-done = s32[128,1,128]{2,1,0:T(1,128)S(1)} async-done(((s32[128,1,128]{2,1,0:T(1,128)}), s32[128,1,128]{2,1,0:T(1,128)S(1)}, u32[]{:S(2)}, u32[]{:S(2)}) %all-to-all-start) | async-done | bytes 65568 | tf_op jit(solution)/shard_map/all_to_all | solution.py:548
  23.3 1.5 %shard_map.159 = f32[2048,128]{1,0:T(8,128)} custom-call(s32[128,128]{1,0:T(8,128)S(1)} %bitcast.16, bf16[256,256]{1,0:T(8,128)(2,1)S(1)} %get-tuple-element.40.blocks_ref), custom_call_target="tpu_custom_call" | custom-call | flops 268435456 | bytes 1048576 | tf_op jit(solution)/shard_map/pallas_call | solution.py:573
  24.9 5.1 %all-to-all-start.1 = ((f32[128,16,128]{2,1,0:T(8,128)}), f32[128,16,128]{2,1,0:T(8,128)S(1)}, u32[]{:S(2)}, u32[]{:S(2)}) async-start(f32[128,16,128]{2,1,0:T(8,128)} %bitcast.6), calls=%async_computation.1 | async-start | bytes 2097152 | tf_op jit(solution)/shard_map/all_to_all | solution.py:586
  30.0 3.4 %copy-done.1 = f32[256,64,128]{2,1,0:T(8,128)S(1)} copy-done((f32[256,64,128]{2,1,0:T(8,128)S(1)}, f32[256,64,128]{2,1,0:T(8,128)}, u32[]{:S(2)}) %copy-start.1) | copy-done | bytes 8388632
  33.4 0.0 copy-start.9
  33.4 1.6 %shard_map.160 = (bf16[16384,256]{1,0:T(8,128)(2,1)S(1)}, f32[256,128]{1,0:T(8,128)S(1)}) custom-call(f32[16384,128]{1,0:T(8,128)S(1)} %bitcast.13), custom_call_target="tpu_custom_call" | custom-call | flops 16777216 | bytes 16777216 | tf_op jit(solution)/shard_map/pallas_call | solution.py:603
  35.0 3.3 %copy-done.6 = bf16[16384,256]{1,0:T(8,128)(2,1)} copy-done((bf16[16384,256]{1,0:T(8,128)(2,1)}, bf16[16384,256]{1,0:T(8,128)(2,1)S(1)}, u32[]{:S(2)}) %copy-start.6) | copy-done | bytes 8388632
  38.3 1.0 %maximum_divide_fusion.incidence_ref = f32[256,128]{1,0:T(8,128)S(1)} fusion(s32[256,128]{1,0:T(8,128)S(1)} %copy-done.11, s32[256,128]{1,0:T(8,128)S(1)} %copy-done.12, f32[256]{0:T(256)S(1)} %copy-done.14, f32[256]{0:T(256)S(1)} %subtract_sqrt_fusion, f32[256]{0:T(256)S(1)} %copy-done.13), kind=kLoop, calls=%fused_computation | loop fusion | flops 360448 | bytes 396288 | tf_op jit(solution)/shard_map/div | solution.py:595
  39.3 9.9 %all-to-all-done.1 = f32[128,16,128]{2,1,0:T(8,128)S(1)} async-done(((f32[128,16,128]{2,1,0:T(8,128)}), f32[128,16,128]{2,1,0:T(8,128)S(1)}, u32[]{:S(2)}, u32[]{:S(2)}) %all-to-all-start.1) | async-done | bytes 1048608 | tf_op jit(solution)/shard_map/all_to_all | solution.py:586
  49.2 9.2 %shard_map.161 = (f32[256,128]{1,0:T(8,128)}, f32[2048,128]{1,0:T(8,128)}) custom-call(f32[2048,128]{1,0:T(8,128)S(1)} %bitcast.15, s32[4,256]{1,0:T(4,128)S(1)} %copy-done.10, s32[256,8]{1,0:T(8,128)S(1)} %copy-done.9, bf16[16384,256]{1,0:T(8,128)(2,1)} %copy-done.6, f32[256,128]{1,0:T(8,128)S(1)} %get-tuple-element.51.inverse_ref, ...), custom_call_target="tpu_custom_call" | custom-call | flops 4294967296 | bytes 8388608 | tf_op jit(solution)/shard_map/pallas_call | solution.py:622
  58.4 4.6 %all-to-all-start.2 = ((f32[128,16,128]{2,1,0:T(8,128)}), f32[128,16,128]{2,1,0:T(8,128)S(1)}, u32[]{:S(2)}, u32[]{:S(2)}) async-start(f32[128,16,128]{2,1,0:T(8,128)} %bitcast.9), calls=%async_computation.2 | async-start | bytes 2097152 | tf_op jit(solution)/shard_map/all_to_all | solution.py:650
  63.1 0.1 shard_map.164.ocean_ref
  63.1 0.0 copy-start
  63.1 2.2 %copy-done = bf16[4096,512]{1,0:T(8,128)(2,1)S(1)} copy-done((bf16[4096,512]{1,0:T(8,128)(2,1)S(1)}, bf16[4096,512]{1,0:T(8,128)(2,1)}, u32[]{:S(2)}) %copy-start) | copy-done | bytes 4194328
  65.3 3.7 %shard_map.162.mixed_ref = bf16[4096,256]{1,0:T(8,128)(2,1)S(1)} custom-call(bf16[4,128,128]{2,1,0:T(8,128)(2,1)S(1)} %copy-done.2, bf16[4096,512]{1,0:T(8,128)(2,1)S(1)} %copy-done), custom_call_target="tpu_custom_call" | custom-call | flops 2147483648 | bytes 4194304 | tf_op jit(solution)/shard_map/pallas_call | solution.py:496
  69.1 4.5 %shard_map.163.kept_ref = bf16[4096,512]{1,0:T(8,128)(2,1)} custom-call(bf16[4,128,128]{2,1,0:T(8,128)(2,1)S(1)} %copy-done.2, bf16[4096,512]{1,0:T(8,128)(2,1)S(1)} %copy-done), custom_call_target="tpu_custom_call" | custom-call | flops 2147483648 | bytes 4194304 | tf_op jit(solution)/shard_map/pallas_call | solution.py:496
  73.6 8.7 %all-to-all-done.2 = f32[128,16,128]{2,1,0:T(8,128)S(1)} async-done(((f32[128,16,128]{2,1,0:T(8,128)}), f32[128,16,128]{2,1,0:T(8,128)S(1)}, u32[]{:S(2)}, u32[]{:S(2)}) %all-to-all-start.2) | async-done | bytes 1048608 | tf_op jit(solution)/shard_map/all_to_all | solution.py:650
  82.3 3.8 %shard_map.165 = (bf16[4096,512]{1,0:T(8,128)(2,1)}, f32[8,4096]{1,0:T(8,128)}) custom-call(f32[2048,128]{1,0:T(8,128)S(1)} %bitcast.14, s32[128,128]{1,0:T(8,128)S(1)} %bitcast.17, f32[8,4096]{1,0:T(8,128)S(1)} %shard_map.164.ocean_ref, bf16[4096,256]{1,0:T(8,128)(2,1)S(1)} %shard_map.162.mixed_ref, ...), custom_call_target="tpu_custom_call", output_to_operand_aliasing={{0}: (4, {})} | custom-call | tf_op jit(solution)/shard_map/pallas_call | solution.py:664
  (23 shorter events, 0.1 us)
Async XLA Ops:
  2.5 20.8 %all-to-all-start = ((s32[128,1,128]{2,1,0:T(1,128)}), s32[128,1,128]{2,1,0:T(1,128)S(1)}, u32[]{:S(2)}, u32[]{:S(2)}) async-start(s32[128,1,128]{2,1,0:T(1,128)} %bitcast.20), calls=%async_computation | async-start | bytes 131072 | tf_op jit(solution)/shard_map/all_to_all | solution.py:548
  14.0 0.8 copy-start.3
  14.8 0.7 copy-start.5
  24.9 24.3 %all-to-all-start.1 = ((f32[128,16,128]{2,1,0:T(8,128)}), f32[128,16,128]{2,1,0:T(8,128)S(1)}, u32[]{:S(2)}, u32[]{:S(2)}) async-start(f32[128,16,128]{2,1,0:T(8,128)} %bitcast.6), calls=%async_computation.1 | async-start | bytes 2097152 | tf_op jit(solution)/shard_map/all_to_all | solution.py:586
  30.0 3.4 %copy-start.1 = (f32[256,64,128]{2,1,0:T(8,128)S(1)}, f32[256,64,128]{2,1,0:T(8,128)}, u32[]{:S(2)}) copy-start(f32[256,64,128]{2,1,0:T(8,128)} %param.21) | copy-start | bytes 25165828
  33.4 4.9 %copy-start.13 = (f32[256]{0:T(256)S(1)}, f32[256]{0:T(256)}, u32[]{:S(2)}) copy-start(f32[256]{0:T(256)} %param.26) | copy-start | bytes 3076
  33.4 4.9 %copy-start.11 = (s32[256,128]{1,0:T(8,128)S(1)}, s32[256,128]{1,0:T(8,128)}, u32[]{:S(2)}) copy-start(s32[256,128]{1,0:T(8,128)} %param.23) | copy-start | bytes 393220
  33.4 4.9 %copy-start.12 = (s32[256,128]{1,0:T(8,128)S(1)}, s32[256,128]{1,0:T(8,128)}, u32[]{:S(2)}) copy-start(s32[256,128]{1,0:T(8,128)} %param.22) | copy-start | bytes 393220
  33.4 4.9 %copy-start.14 = (f32[256]{0:T(256)S(1)}, f32[256]{0:T(256)}, u32[]{:S(2)}) copy-start(f32[256]{0:T(256)} %param.27) | copy-start | bytes 3076
  33.4 15.8 %copy-start.7 = (f32[256,128]{1,0:T(8,128)S(1)}, f32[256,128]{1,0:T(8,128)}, u32[]{:S(2)}) copy-start(f32[256,128]{1,0:T(8,128)} %sky_ref.1) | copy-start | bytes 393220
  33.4 15.8 %copy-start.8 = (f32[256,128]{1,0:T(8,128)S(1)}, f32[256,128]{1,0:T(8,128)}, u32[]{:S(2)}) copy-start(f32[256,128]{1,0:T(8,128)} %albedo_ref.1) | copy-start | bytes 393220
  33.4 15.8 %copy-start.9 = (s32[256,8]{1,0:T(8,128)S(1)}, s32[256,8]{1,0:T(8,128)}, u32[]{:S(2)}) copy-start(s32[256,8]{1,0:T(8,128)} %get-tuple-element.49.col_ref) | copy-start | bytes 24580
  33.4 15.7 %copy-start.10 = (s32[4,256]{1,0:T(4,128)S(1)}, s32[4,256]{1,0:T(4,128)}, u32[]{:S(2)}) copy-start(s32[4,256]{1,0:T(4,128)} %get-tuple-element.48.row_ref) | copy-start | bytes 12292
  35.0 3.3 %copy-start.6 = (bf16[16384,256]{1,0:T(8,128)(2,1)}, bf16[16384,256]{1,0:T(8,128)(2,1)S(1)}, u32[]{:S(2)}) copy-start(bf16[16384,256]{1,0:T(8,128)(2,1)S(1)} %get-tuple-element.50.both_ref) | copy-start | bytes 25165828
  49.2 13.9 %copy-start.4 = (s32[4096]{0:T(1024)S(1)}, s32[4096]{0:T(1024)}, u32[]{:S(2)}) copy-start(s32[4096]{0:T(1024)} %param.18) | copy-start | bytes 49156
  49.2 13.9 %copy-start.2 = (bf16[4,128,128]{2,1,0:T(8,128)(2,1)S(1)}, bf16[4,128,128]{2,1,0:T(8,128)(2,1)}, u32[]{:S(2)}) copy-start(bf16[4,128,128]{2,1,0:T(8,128)(2,1)} %mixing_ref.3) | copy-start | bytes 393220
  58.4 23.9 %all-to-all-start.2 = ((f32[128,16,128]{2,1,0:T(8,128)}), f32[128,16,128]{2,1,0:T(8,128)S(1)}, u32[]{:S(2)}, u32[]{:S(2)}) async-start(f32[128,16,128]{2,1,0:T(8,128)} %bitcast.9), calls=%async_computation.2 | async-start | bytes 2097152 | tf_op jit(solution)/shard_map/all_to_all | solution.py:650
  63.1 2.2 %copy-start = (bf16[4096,512]{1,0:T(8,128)(2,1)S(1)}, bf16[4096,512]{1,0:T(8,128)(2,1)}, u32[]{:S(2)}) copy-start(bf16[4096,512]{1,0:T(8,128)(2,1)} %state_ref.2) | copy-start | bytes 12582916

commit v4 on v3

--- a/solution.py
+++ b/solution.py
@@ -565,7 +565,7 @@
             pltpu.VMEM((columns, NV * LEV), BF16),
             pltpu.SemaphoreType.DMA((parts,)),
         ],
-        compiler_params=params(50, 1),
+        compiler_params=params(58, 1),
         cost_estimate=cost(columns * 512 * 32 * 2, columns * 1024),
     )(profile.reshape(1, LEV), atm_state, radiation)
     incoming, forcing, blocks = lax.optimization_barrier((incoming, forcing, blocks))
@@ -577,7 +577,7 @@
         out_specs=pl.BlockSpec(memory_space=pltpu.HBM),
         out_shape=jax.ShapeDtypeStruct((slots, 128), F32),
         scratch_shapes=[pltpu.VMEM((slots, 128), F32), pltpu.SemaphoreType.DMA((4,))],
-        compiler_params=params(16, 1),
+        compiler_params=params(60, 1),
         cost_estimate=cost(slots * 256 * 256 * 2, slots * 512),
     )(incoming, blocks)
     reply, remap_w, slope_class, sun_cos = lax.optimization_barrier(

time: 86.7 us -> 88.3 us (1.018)
  Pallas kernels: 29.4 us -> 31.9 us
  local copies, waits for them, and re-layouts: 10.4 us -> 9.51 us
    pallas_call x1, Pallas kernels: 3.16 us -> 4.68 us  [on_device(): pl.pallas_call(forcing_kernel, grid=(1,), in_specs=[whole(1, LEV), pl.Blo...]
    pallas_call x1, Pallas kernels: 1.53 us -> 2.47 us  [on_device(): pl.pallas_call(reply_kernel, grid=(1,), in_specs=[whole(devices, 128), wh...]
    unnamed x30 -> x32, local copies, waits for them, and re-layouts: 10.4 us -> 9.51 us
  transfers between devices with their start and end apart: 3 -> 3, of which waited for: 3 -> 3; matrix products, arithmetic and copies ran while one was open for 1% -> 1% of each run, Pallas kernels for 15% -> 17%
where the time goes in v4:
time: 88.3 us; the launch traced here: 87.9 us
  Pallas kernels  31.9 us (36%)
  waiting for transfers between devices  23.2 us (26%)
  starting transfers between devices  21.3 us (24%)
  local copies, waits for them, and re-layouts  9.51 us (11%)
  between operations  1.03 us (1%)
  other arithmetic  0.97 us (1%)
    all_to_all x1, starting transfers between devices, on_device(): lax.all_to_all(wanted, AXES, split_axis=0, concat_axis=0, tiled=True)  11.5 us
    all_to_all x1, waiting for transfers between devices, on_device(): lax.all_to_all(reply.reshape(devices, CAP, 128), AXES, split_axis=0, conc...  9.87 us
    unnamed x32, local copies, waits for them, and re-layouts  9.51 us
    pallas_call x1, Pallas kernels, on_device(): pl.pallas_call(land_kernel, grid=(1,), in_specs=[whole(slots, 128), whole...  9.22 us
    all_to_all x1, waiting for transfers between devices, on_device(): lax.all_to_all(outgoing.reshape(devices, CAP, 128), AXES, split_axis=0, c...  8.7 us
    pallas_call x2, Pallas kernels, mix(): pl.pallas_call(functools.partial(mix_kernel, half, out_half), grid=(1,),...  8.29 us
    all_to_all x1, starting transfers between devices, on_device(): lax.all_to_all(reply.reshape(devices, CAP, 128), AXES, split_axis=0, conc...  5.13 us
    pallas_call x1, Pallas kernels, on_device(): pl.pallas_call(forcing_kernel, grid=(1,), in_specs=[whole(1, LEV), pl.Blo...  4.68 us
  transfers between devices with their start and end apart: 3, of which 3 were waited for; matrix products, arithmetic and copies ran while one was open for 1% of the time, Pallas kernels for 17%

profile of v4, /device:TPU:1, one launch (start us, length us, event | category | flops | bytes accessed | tf_op | source)
XLA Modules:
  0.0 87.9 jit_solution(16145615054125959454)
XLA Ops:
  0.6 1.9 %shard_map.157 = (s32[128,128]{1,0:T(8,128)}, s32[4,256]{1,0:T(4,128)}, s32[256,8]{1,0:T(8,128)}) custom-call(s32[4,256]{1,0:T(4,128)} %bitcast.21, s32[4,256]{1,0:T(4,128)} %bitcast.22), custom_call_target="tpu_custom_call" | custom-call | tf_op jit(solution)/shard_map/pallas_call | solution.py:538
  2.5 11.5 %all-to-all-start = ((s32[128,1,128]{2,1,0:T(1,128)}), s32[128,1,128]{2,1,0:T(1,128)S(1)}, u32[]{:S(2)}, u32[]{:S(2)}) async-start(s32[128,1,128]{2,1,0:T(1,128)} %bitcast.20), calls=%async_computation | async-start | bytes 131072 | tf_op jit(solution)/shard_map/all_to_all | solution.py:548
  14.0 4.7 %shard_map.158 = (f32[8,4096]{1,0:T(8,128)}, bf16[256,256]{1,0:T(8,128)(2,1)}) custom-call(f32[1,128]{1,0:T(1,128)} %bitcast.23, bf16[4096,512]{1,0:T(8,128)(2,1)} %state_ref.2, f32[4,4096]{1,0:T(4,128)} %radiation_ref.1), custom_call_target="tpu_custom_call" | custom-call | flops 134217728 | bytes 4194304 | tf_op jit(solution)/shard_map/pallas_call | solution.py:551
  18.7 4.6 %all-to-all-done = s32[128,1,128]{2,1,0:T(1,128)S(1)} async-done(((s32[128,1,128]{2,1,0:T(1,128)}), s32[128,1,128]{2,1,0:T(1,128)S(1)}, u32[]{:S(2)}, u32[]{:S(2)}) %all-to-all-start) | async-done | bytes 65568 | tf_op jit(solution)/shard_map/all_to_all | solution.py:548
  23.3 0.6 copy-done.2
  24.0 2.5 %shard_map.159 = f32[2048,128]{1,0:T(8,128)} custom-call(s32[128,128]{1,0:T(8,128)} %bitcast.16, bf16[256,256]{1,0:T(8,128)(2,1)} %get-tuple-element.40.blocks_ref), custom_call_target="tpu_custom_call" | custom-call | flops 268435456 | bytes 1048576 | tf_op jit(solution)/shard_map/pallas_call | solution.py:573
  26.4 5.1 %all-to-all-start.1 = ((f32[128,16,128]{2,1,0:T(8,128)}), f32[128,16,128]{2,1,0:T(8,128)S(1)}, u32[]{:S(2)}, u32[]{:S(2)}) async-start(f32[128,16,128]{2,1,0:T(8,128)} %bitcast.19), calls=%async_computation.1 | async-start | bytes 2097152 | tf_op jit(solution)/shard_map/all_to_all | solution.py:586
  31.6 0.0 copy-start.1
  31.6 3.4 %copy-done.1 = f32[256,64,128]{2,1,0:T(8,128)S(1)} copy-done((f32[256,64,128]{2,1,0:T(8,128)S(1)}, f32[256,64,128]{2,1,0:T(8,128)}, u32[]{:S(2)}) %copy-start.1) | copy-done | bytes 8388632
  35.0 0.0 copy-start.8
  35.0 0.0 copy-start.9
  35.0 1.6 %shard_map.160 = (bf16[16384,256]{1,0:T(8,128)(2,1)S(1)}, f32[256,128]{1,0:T(8,128)S(1)}) custom-call(f32[16384,128]{1,0:T(8,128)S(1)} %bitcast.13), custom_call_target="tpu_custom_call" | custom-call | flops 16777216 | bytes 16777216 | tf_op jit(solution)/shard_map/pallas_call | solution.py:603
  36.6 3.3 %copy-done.7 = bf16[16384,256]{1,0:T(8,128)(2,1)} copy-done((bf16[16384,256]{1,0:T(8,128)(2,1)}, bf16[16384,256]{1,0:T(8,128)(2,1)S(1)}, u32[]{:S(2)}) %copy-start.7) | copy-done | bytes 8388632
  39.9 1.0 %maximum_divide_fusion.incidence_ref = f32[256,128]{1,0:T(8,128)S(1)} fusion(s32[256,128]{1,0:T(8,128)S(1)} %copy-done.12, s32[256,128]{1,0:T(8,128)S(1)} %copy-done.13, f32[256]{0:T(256)S(1)} %copy-done.15, f32[256]{0:T(256)S(1)} %subtract_sqrt_fusion, f32[256]{0:T(256)S(1)} %copy-done.14), kind=kLoop, calls=%fused_computation | loop fusion | flops 360448 | bytes 396288 | tf_op jit(solution)/shard_map/div | solution.py:595
  40.9 9.9 %all-to-all-done.1 = f32[128,16,128]{2,1,0:T(8,128)S(1)} async-done(((f32[128,16,128]{2,1,0:T(8,128)}), f32[128,16,128]{2,1,0:T(8,128)S(1)}, u32[]{:S(2)}, u32[]{:S(2)}) %all-to-all-start.1) | async-done | bytes 1048608 | tf_op jit(solution)/shard_map/all_to_all | solution.py:586
  50.8 0.0 copy-start.6
  50.8 9.2 %shard_map.161 = (f32[256,128]{1,0:T(8,128)}, f32[2048,128]{1,0:T(8,128)}) custom-call(f32[2048,128]{1,0:T(8,128)S(1)} %bitcast.15, s32[4,256]{1,0:T(4,128)S(1)} %copy-done.11, s32[256,8]{1,0:T(8,128)S(1)} %copy-done.10, bf16[16384,256]{1,0:T(8,128)(2,1)} %copy-done.7, f32[256,128]{1,0:T(8,128)S(1)} %get-tuple-element.51.inverse_ref, ...), custom_call_target="tpu_custom_call" | custom-call | flops 4294967296 | bytes 8388608 | tf_op jit(solution)/shard_map/pallas_call | solution.py:622
  60.0 4.6 %all-to-all-start.2 = ((f32[128,16,128]{2,1,0:T(8,128)}), f32[128,16,128]{2,1,0:T(8,128)S(1)}, u32[]{:S(2)}, u32[]{:S(2)}) async-start(f32[128,16,128]{2,1,0:T(8,128)} %bitcast.9), calls=%async_computation.2 | async-start | bytes 2097152 | tf_op jit(solution)/shard_map/all_to_all | solution.py:650
  64.7 0.1 shard_map.164.ocean_ref
  64.8 2.2 %copy-done = bf16[4096,512]{1,0:T(8,128)(2,1)S(1)} copy-done((bf16[4096,512]{1,0:T(8,128)(2,1)S(1)}, bf16[4096,512]{1,0:T(8,128)(2,1)}, u32[]{:S(2)}) %copy-start) | copy-done | bytes 4194328
  67.0 3.7 %shard_map.162.mixed_ref = bf16[4096,256]{1,0:T(8,128)(2,1)S(1)} custom-call(bf16[4,128,128]{2,1,0:T(8,128)(2,1)S(1)} %copy-done.4, bf16[4096,512]{1,0:T(8,128)(2,1)S(1)} %copy-done), custom_call_target="tpu_custom_call" | custom-call | flops 2147483648 | bytes 4194304 | tf_op jit(solution)/shard_map/pallas_call | solution.py:496
  70.7 4.5 %shard_map.163.kept_ref = bf16[4096,512]{1,0:T(8,128)(2,1)} custom-call(bf16[4,128,128]{2,1,0:T(8,128)(2,1)S(1)} %copy-done.4, bf16[4096,512]{1,0:T(8,128)(2,1)S(1)} %copy-done), custom_call_target="tpu_custom_call" | custom-call | flops 2147483648 | bytes 4194304 | tf_op jit(solution)/shard_map/pallas_call | solution.py:496
  75.3 8.7 %all-to-all-done.2 = f32[128,16,128]{2,1,0:T(8,128)S(1)} async-done(((f32[128,16,128]{2,1,0:T(8,128)}), f32[128,16,128]{2,1,0:T(8,128)S(1)}, u32[]{:S(2)}, u32[]{:S(2)}) %all-to-all-start.2) | async-done | bytes 1048608 | tf_op jit(solution)/shard_map/all_to_all | solution.py:650
  84.0 3.8 %shard_map.165 = (bf16[4096,512]{1,0:T(8,128)(2,1)}, f32[8,4096]{1,0:T(8,128)}) custom-call(f32[2048,128]{1,0:T(8,128)S(1)} %bitcast.14, s32[128,128]{1,0:T(8,128)S(1)} %bitcast.17, f32[8,4096]{1,0:T(8,128)S(1)} %shard_map.164.ocean_ref, bf16[4096,256]{1,0:T(8,128)(2,1)S(1)} %shard_map.162.mixed_ref, ...), custom_call_target="tpu_custom_call", output_to_operand_aliasing={{0}: (4, {})} | custom-call | tf_op jit(solution)/shard_map/pallas_call | solution.py:664
  (25 shorter events, 0.1 us)
Async XLA Ops:
  2.5 20.8 %all-to-all-start = ((s32[128,1,128]{2,1,0:T(1,128)}), s32[128,1,128]{2,1,0:T(1,128)S(1)}, u32[]{:S(2)}, u32[]{:S(2)}) async-start(s32[128,1,128]{2,1,0:T(1,128)} %bitcast.20), calls=%async_computation | async-start | bytes 131072 | tf_op jit(solution)/shard_map/all_to_all | solution.py:548
  23.3 0.6 copy-start.2
  26.4 24.3 %all-to-all-start.1 = ((f32[128,16,128]{2,1,0:T(8,128)}), f32[128,16,128]{2,1,0:T(8,128)S(1)}, u32[]{:S(2)}, u32[]{:S(2)}) async-start(f32[128,16,128]{2,1,0:T(8,128)} %bitcast.19), calls=%async_computation.1 | async-start | bytes 2097152 | tf_op jit(solution)/shard_map/all_to_all | solution.py:586
  31.6 3.4 %copy-start.1 = (f32[256,64,128]{2,1,0:T(8,128)S(1)}, f32[256,64,128]{2,1,0:T(8,128)}, u32[]{:S(2)}) copy-start(f32[256,64,128]{2,1,0:T(8,128)} %param.21) | copy-start | bytes 25165828
  35.0 4.9 %copy-start.14 = (f32[256]{0:T(256)S(1)}, f32[256]{0:T(256)}, u32[]{:S(2)}) copy-start(f32[256]{0:T(256)} %param.26) | copy-start | bytes 3076
  35.0 4.9 %copy-start.12 = (s32[256,128]{1,0:T(8,128)S(1)}, s32[256,128]{1,0:T(8,128)}, u32[]{:S(2)}) copy-start(s32[256,128]{1,0:T(8,128)} %param.23) | copy-start | bytes 393220
  35.0 4.9 %copy-start.13 = (s32[256,128]{1,0:T(8,128)S(1)}, s32[256,128]{1,0:T(8,128)}, u32[]{:S(2)}) copy-start(s32[256,128]{1,0:T(8,128)} %param.22) | copy-start | bytes 393220
  35.0 4.9 %copy-start.15 = (f32[256]{0:T(256)S(1)}, f32[256]{0:T(256)}, u32[]{:S(2)}) copy-start(f32[256]{0:T(256)} %param.27) | copy-start | bytes 3076
  35.0 15.8 %copy-start.8 = (f32[256,128]{1,0:T(8,128)S(1)}, f32[256,128]{1,0:T(8,128)}, u32[]{:S(2)}) copy-start(f32[256,128]{1,0:T(8,128)} %sky_ref.1) | copy-start | bytes 393220
  35.0 15.8 %copy-start.9 = (f32[256,128]{1,0:T(8,128)S(1)}, f32[256,128]{1,0:T(8,128)}, u32[]{:S(2)}) copy-start(f32[256,128]{1,0:T(8,128)} %albedo_ref.1) | copy-start | bytes 393220
  35.0 15.8 %copy-start.10 = (s32[256,8]{1,0:T(8,128)S(1)}, s32[256,8]{1,0:T(8,128)}, u32[]{:S(2)}) copy-start(s32[256,8]{1,0:T(8,128)} %get-tuple-element.49.col_ref) | copy-start | bytes 24580
  35.0 15.7 %copy-start.11 = (s32[4,256]{1,0:T(4,128)S(1)}, s32[4,256]{1,0:T(4,128)}, u32[]{:S(2)}) copy-start(s32[4,256]{1,0:T(4,128)} %get-tuple-element.48.row_ref) | copy-start | bytes 12292
  36.6 3.3 %copy-start.7 = (bf16[16384,256]{1,0:T(8,128)(2,1)}, bf16[16384,256]{1,0:T(8,128)(2,1)S(1)}, u32[]{:S(2)}) copy-start(bf16[16384,256]{1,0:T(8,128)(2,1)S(1)} %get-tuple-element.50.both_ref) | copy-start | bytes 25165828
  50.8 13.9 %copy-start.5 = (f32[8,4096]{1,0:T(8,128)S(1)}, f32[8,4096]{1,0:T(8,128)}, u32[]{:S(2)}) copy-start(f32[8,4096]{1,0:T(8,128)} %get-tuple-element.57.forcing_ref) | copy-start | bytes 393220
  50.8 13.9 %copy-start.6 = (s32[4096]{0:T(1024)S(1)}, s32[4096]{0:T(1024)}, u32[]{:S(2)}) copy-start(s32[4096]{0:T(1024)} %param.18) | copy-start | bytes 49156
  50.8 14.0 %copy-start.4 = (bf16[4,128,128]{2,1,0:T(8,128)(2,1)S(1)}, bf16[4,128,128]{2,1,0:T(8,128)(2,1)}, u32[]{:S(2)}) copy-start(bf16[4,128,128]{2,1,0:T(8,128)(2,1)} %mixing_ref.3) | copy-start | bytes 393220
  60.0 23.9 %all-to-all-start.2 = ((f32[128,16,128]{2,1,0:T(8,128)}), f32[128,16,128]{2,1,0:T(8,128)S(1)}, u32[]{:S(2)}, u32[]{:S(2)}) async-start(f32[128,16,128]{2,1,0:T(8,128)} %bitcast.9), calls=%async_computation.2 | async-start | bytes 2097152 | tf_op jit(solution)/shard_map/all_to_all | solution.py:650
  64.8 2.2 %copy-start = (bf16[4096,512]{1,0:T(8,128)(2,1)S(1)}, bf16[4096,512]{1,0:T(8,128)(2,1)}, u32[]{:S(2)}) copy-start(bf16[4096,512]{1,0:T(8,128)(2,1)} %state_ref.2) | copy-start | bytes 12582916
  70.7 13.3 %copy-start.3 = (s32[128,1,128]{2,1,0:T(1,128)S(1)}, s32[128,1,128]{2,1,0:T(1,128)}, u32[]{:S(2)}) copy-start(s32[128,1,128]{2,1,0:T(1,128)} %copy-done.2) | copy-start | bytes 196612
